TPU v7x, 32 devices: a whole 2x2x4 slice. The times are simulated.
32 devices in a mesh: dp: 16 (over z, y, x), tensor: 2 (over core).
Axes of the slice: x: 2, y: 2, z: 4, core: 2. Of those that a mesh axis runs over, the one named last changes fastest.
Arguments:
- states: bfloat16 [71680, 512], P(('dp', 'tensor')), may hold values from -6 to 6
- cotangent: bfloat16 [71680, 512], P(('dp', 'tensor')), may hold values from -6 to 6
- lengths: int32 [448], P('dp'), may hold values from 100 to 160, as said below
- span_starts: int32 [448], P('dp'), may hold values from 0 to 80, as said below
- span_ends: int32 [448], P('dp'), may hold values from 1 to 160, as said below
- query_weight: bfloat16 [512, 512], P(None, 'tensor'), may hold values from -0.375 to 0.375
- query_bias: bfloat16 [512], P('tensor'), may hold values from -3 to 3
- key_weight: bfloat16 [512, 512], P(None, 'tensor'), may hold values from -0.375 to 0.375
- value_weight: bfloat16 [512, 512], P(None, 'tensor'), may hold values from -0.25 to 0.25
- value_bias: bfloat16 [512], P('tensor'), may hold values from -3 to 3
- output_weight: bfloat16 [512, 512], P('tensor'), may hold values from -1 to 1
- output_bias: bfloat16 [512], replicated, may hold values from -3 to 3
- first_gain: bfloat16 [512], replicated, may hold values from 0.25 to 1.75
- first_shift: bfloat16 [512], replicated, may hold values from -3 to 3
- inner_weight: bfloat16 [512, 2048], P(None, 'tensor'), may hold values from -0.25 to 0.25
- inner_bias: bfloat16 [2048], P('tensor'), may hold values from -3 to 3
- down_weight: bfloat16 [2048, 512], P('tensor'), may hold values from -0.125 to 0.125
- down_bias: bfloat16 [512], replicated, may hold values from -3 to 3
- second_gain: bfloat16 [512], replicated, may hold values from 0.25 to 1.75
- second_shift: bfloat16 [512], replicated, may hold values from -3 to 3
Outputs:
- layer_out: bfloat16 [71680, 512], P(('dp', 'tensor'))
- input_grad: float32 [71680, 512], P(('dp', 'tensor'))
- query_weight_grad: float32 [512, 512], P(None, 'tensor')
- query_bias_grad: float32 [512], P('tensor')
- key_weight_grad: float32 [512, 512], P(None, 'tensor')
- value_weight_grad: float32 [512, 512], P(None, 'tensor')
- value_bias_grad: float32 [512], P('tensor')
- output_weight_grad: float32 [512, 512], P('tensor')
- output_bias_grad: float32 [512], replicated
- first_gain_grad: float32 [512], replicated
- first_shift_grad: float32 [512], replicated
- inner_weight_grad: float32 [512, 2048], P(None, 'tensor')
- inner_bias_grad: float32 [2048], P('tensor')
- down_weight_grad: float32 [2048, 512], P('tensor')
- down_bias_grad: float32 [512], replicated
- second_gain_grad: float32 [512], replicated
- second_shift_grad: float32 [512], replicated
Inputs may be any that keep to these rules, and one draw needn't show every extreme that they name: `lengths`: in every aligned block of 28 chains one chain has all 160 positions. `span_starts`: at most half of the chain's length; 0 for the full chain of each block. `span_ends`: after the span's start and within the chain's length; the full chain of each block is masked whole.
All inputs are finite; a program needn't handle non-finite values.
Results may differ from a plain program's by a relative error of at most 0.02.
Values may be sent and summed in bfloat16 or wider, within the bound.
A program may use at most 256 MiB of HBM per device.

v0:
```python
import jax
import jax.numpy as jnp
from jax import lax
from jax.sharding import PartitionSpec as P

HEAD_DIM = 64
SEQ = 160


EPSILON = 1e-12


def product(left, right):
    return jnp.dot(left, right, preferred_element_type=jnp.float32)


def product_left(left, right):
    return lax.dot_general(
        left, right, (((0,), (0,)), ((), ())), preferred_element_type=jnp.float32
    )


def product_right(left, right):
    return lax.dot_general(
        left, right, (((1,), (1,)), ((), ())), preferred_element_type=jnp.float32
    )


def layer_norm(values, gain, shift):
    center = values - jnp.mean(values, axis=-1, keepdims=True)
    spread = jnp.mean(center * center, axis=-1, keepdims=True)
    return center * lax.rsqrt(spread + EPSILON) * gain + shift


def exact_gelu(values):
    return jax.nn.gelu(values, approximate=False)


def attention_scores(queries, keys, key_live):
    scores = jnp.einsum(
        "cqhd,ckhd->chqk", queries, keys, preferred_element_type=jnp.float32
    ) * HEAD_DIM ** (-0.5)
    return jnp.where(key_live[:, None, None, :], scores, -1000000000.0)


def per_row(table, picker):
    return jnp.sum(jnp.where(picker, table[None, :], 0), axis=1)


def column_sum(values):
    return jnp.sum(values.astype(jnp.float32), axis=0)


def local(
    states,
    cotangent,
    lengths,
    span_starts,
    span_ends,
    query_weight,
    query_bias,
    key_weight,
    value_weight,
    value_bias,
    output_weight,
    output_bias,
    first_gain,
    first_shift,
    inner_weight,
    inner_bias,
    down_weight,
    down_bias,
    second_gain,
    second_shift,
):
    slice_rows = states.shape[0]
    chains = lengths.shape[0]
    group_rows = chains * SEQ
    heads_local = query_weight.shape[1] // HEAD_DIM
    layout = (chains, SEQ, heads_local, HEAD_DIM)
    whole = lax.all_gather(states, "tensor", axis=0, tiled=True)
    queries = (product(whole, query_weight) + query_bias).astype(jnp.bfloat16).reshape(layout)
    keys_low = product(whole, key_weight).astype(jnp.bfloat16).reshape(layout)
    values_low = (product(whole, value_weight) + value_bias).astype(jnp.bfloat16).reshape(layout)
    key_live = jnp.arange(SEQ, dtype=jnp.int32)[None, :] < lengths[:, None]
    scores = attention_scores(queries, keys_low, key_live)
    highest = jnp.max(scores, axis=-1, keepdims=True)
    logsum = highest + jnp.log(jnp.sum(jnp.exp(scores - highest), axis=-1, keepdims=True))
    probs_low = jnp.exp(scores - logsum).astype(jnp.bfloat16)
    context = jnp.einsum(
        "chqk,ckhd->cqhd", probs_low, values_low, preferred_element_type=jnp.float32
    )
    context = context.reshape(group_rows, heads_local * HEAD_DIM).astype(jnp.bfloat16)
    attended = lax.psum_scatter(
        product(context, output_weight), "tensor", scatter_dimension=0, tiled=True
    ) + output_bias.astype(jnp.float32)
    first_sum = states.astype(jnp.float32) + attended
    normed, first_pull = jax.vjp(
        layer_norm, first_sum, first_gain.astype(jnp.float32), first_shift.astype(jnp.float32)
    )
    normed_low = normed.astype(jnp.bfloat16)
    normed_all = lax.all_gather(normed_low, "tensor", axis=0, tiled=True)
    hidden = product(normed_all, inner_weight) + inner_bias.astype(jnp.float32)
    activation, gelu_pull = jax.vjp(exact_gelu, hidden)
    activation_low = activation.astype(jnp.bfloat16)
    branch = lax.psum_scatter(
        product(activation_low, down_weight), "tensor", scatter_dimension=0, tiled=True
    )
    second_sum = normed + (branch + down_bias.astype(jnp.float32))
    output, second_pull = jax.vjp(
        layer_norm, second_sum, second_gain.astype(jnp.float32), second_shift.astype(jnp.float32)
    )
    row_ids = lax.axis_index("tensor") * slice_rows + jnp.arange(slice_rows, dtype=jnp.int32)
    chain_ids = row_ids // SEQ
    position = row_ids % SEQ
    picker = chain_ids[:, None] == jnp.arange(chains, dtype=jnp.int32)[None, :]
    live = (
        (position >= per_row(span_starts, picker))
        & (position < per_row(span_ends, picker))
        & (position < per_row(lengths, picker))
    )
    grad_out = jnp.where(live[:, None], cotangent.astype(jnp.float32), 0.0)
    grad_second, second_gain_part, second_shift_part = second_pull(grad_out)
    grad_branch = grad_second.astype(jnp.bfloat16)
    down_bias_part = column_sum(grad_branch)
    grad_branch_all = lax.all_gather(grad_branch, "tensor", axis=0, tiled=True)
    down_weight_part = product_left(activation_low, grad_branch_all)
    grad_activation = product_right(grad_branch_all, down_weight)
    (grad_hidden,) = gelu_pull(grad_activation)
    grad_hidden_low = grad_hidden.astype(jnp.bfloat16)
    inner_weight_part = product_left(normed_all, grad_hidden_low)
    inner_bias_part = column_sum(grad_hidden_low)
    grad_normed = lax.psum_scatter(
        product_right(grad_hidden_low, inner_weight), "tensor", scatter_dimension=0, tiled=True
    )
    grad_first, first_gain_part, first_shift_part = first_pull(grad_second + grad_normed)
    grad_attended = grad_first.astype(jnp.bfloat16)
    output_bias_part = column_sum(grad_attended)
    grad_attended_all = lax.all_gather(grad_attended, "tensor", axis=0, tiled=True)
    output_weight_part = product_left(context, grad_attended_all)
    grad_context = (
        product_right(grad_attended_all, output_weight).astype(jnp.bfloat16).reshape(layout)
    )
    probs = jnp.exp(attention_scores(queries, keys_low, key_live) - logsum)
    grad_probs = jnp.einsum(
        "cqhd,ckhd->chqk", grad_context, values_low, preferred_element_type=jnp.float32
    )
    grad_scores = probs * (grad_probs - jnp.sum(probs * grad_probs, axis=-1, keepdims=True))
    grad_scores_low = grad_scores.astype(jnp.bfloat16)
    scale = HEAD_DIM ** (-0.5)
    grad_queries = (
        jnp.einsum("chqk,ckhd->cqhd", grad_scores_low, keys_low, preferred_element_type=jnp.float32)
        * scale
    )
    grad_keys = (
        jnp.einsum("chqk,cqhd->ckhd", grad_scores_low, queries, preferred_element_type=jnp.float32)
        * scale
    )
    grad_values = jnp.einsum(
        "chqk,cqhd->ckhd", probs_low, grad_context, preferred_element_type=jnp.float32
    )
    flat = (group_rows, heads_local * HEAD_DIM)
    grad_queries = grad_queries.reshape(flat).astype(jnp.bfloat16)
    grad_keys = grad_keys.reshape(flat).astype(jnp.bfloat16)
    grad_values = grad_values.reshape(flat).astype(jnp.bfloat16)
    query_weight_part = product_left(whole, grad_queries)
    key_weight_part = product_left(whole, grad_keys)
    value_weight_part = product_left(whole, grad_values)
    query_bias_part = column_sum(grad_queries)
    value_bias_part = column_sum(grad_values)
    grad_whole = (
        product_right(grad_queries, query_weight)
        + product_right(grad_keys, key_weight)
        + product_right(grad_values, value_weight)
    )
    input_grad = (
        lax.psum_scatter(
            grad_whole.astype(jnp.bfloat16), "tensor", scatter_dimension=0, tiled=True
        ).astype(jnp.float32)
        + grad_first
    )
    (
        query_weight_grad,
        query_bias_grad,
        key_weight_grad,
        value_weight_grad,
        value_bias_grad,
        output_weight_grad,
        inner_weight_grad,
        inner_bias_grad,
        down_weight_grad,
    ) = (
        lax.psum(query_weight_part.astype(jnp.bfloat16), "dp").astype(jnp.float32),
        lax.psum(query_bias_part.astype(jnp.bfloat16), "dp").astype(jnp.float32),
        lax.psum(key_weight_part.astype(jnp.bfloat16), "dp").astype(jnp.float32),
        lax.psum(value_weight_part.astype(jnp.bfloat16), "dp").astype(jnp.float32),
        lax.psum(value_bias_part.astype(jnp.bfloat16), "dp").astype(jnp.float32),
        lax.psum(output_weight_part.astype(jnp.bfloat16), "dp").astype(jnp.float32),
        lax.psum(inner_weight_part.astype(jnp.bfloat16), "dp").astype(jnp.float32),
        lax.psum(inner_bias_part.astype(jnp.bfloat16), "dp").astype(jnp.float32),
        lax.psum(down_weight_part.astype(jnp.bfloat16), "dp").astype(jnp.float32),
    )
    (
        output_bias_grad,
        first_gain_grad,
        first_shift_grad,
        down_bias_grad,
        second_gain_grad,
        second_shift_grad,
    ) = lax.psum(
        (
            output_bias_part,
            first_gain_part,
            first_shift_part,
            down_bias_part,
            second_gain_part,
            second_shift_part,
        ),
        ("dp", "tensor"),
    )
    return (
        output.astype(jnp.bfloat16),
        input_grad,
        query_weight_grad,
        query_bias_grad,
        key_weight_grad,
        value_weight_grad,
        value_bias_grad,
        output_weight_grad,
        output_bias_grad,
        first_gain_grad,
        first_shift_grad,
        inner_weight_grad,
        inner_bias_grad,
        down_weight_grad,
        down_bias_grad,
        second_gain_grad,
        second_shift_grad,
    )


def solution(mesh):
    placed = (
        P(("dp", "tensor"), None),
        P(("dp", "tensor"), None),
        P("dp"),
        P("dp"),
        P("dp"),
        P(None, "tensor"),
        P("tensor"),
        P(None, "tensor"),
        P(None, "tensor"),
        P("tensor"),
        P("tensor", None),
        P(),
        P(),
        P(),
        P(None, "tensor"),
        P("tensor"),
        P("tensor", None),
        P(),
        P(),
        P(),
    )
    return jax.shard_map(
        local,
        mesh=mesh,
        in_specs=placed,
        out_specs=(
            P(("dp", "tensor"), None),
            P(("dp", "tensor"), None),
            P(None, "tensor"),
            P("tensor"),
            P(None, "tensor"),
            P(None, "tensor"),
            P("tensor"),
            P("tensor", None),
            P(),
            P(),
            P(),
            P(None, "tensor"),
            P("tensor"),
            P("tensor", None),
            P(),
            P(),
            P(),
        ),
        check_vma=False,
    )
```

profile of v0, /device:TPU:0, one launch (start us, length us, event | category | flops | bytes accessed | tf_op | source)
XLA Modules:
  0.0 662.7 jit_solution(7857392860595286431)
XLA Ops:
  10.0 16.5 %all-gather.5.cloned.1.call-done = bf16[4480,512]{1,0:T(8,128)(2,1)} async-done(((bf16[2240,512]{1,0:T(8,128)(2,1)}), bf16[4480,512]{1,0:T(8,128)(2,1)}) %all-gather.5.cloned.1.call-update) | async-done | bytes 4587536 | tf_op jit(solution)/shard_map/all_gather | solution.py:81
  34.1 8.4 %copy.78 = bf16[28,160,4,64]{1,3,2,0:T(8,128)(2,1)} copy(bf16[28,160,4,64]{3,2,1,0:T(4,128)(2,1)} %reshape.189) | data formatting | bytes 4587520 | tf_op jit(solution)/shard_map/reshape | solution.py:82
  50.1 8.4 %copy.80 = bf16[28,160,4,64]{1,3,2,0:T(8,128)(2,1)} copy(bf16[28,160,4,64]{3,2,1,0:T(4,128)(2,1)} %reshape.188) | data formatting | bytes 4587520 | tf_op jit(solution)/shard_map/reshape | solution.py:84
  66.1 8.4 %copy.79 = bf16[28,160,4,64]{1,3,2,0:T(8,128)(2,1)} copy(bf16[28,160,4,64]{3,2,1,0:T(4,128)(2,1)} %reshape.190) | data formatting | bytes 4587520 | tf_op jit(solution)/shard_map/reshape | solution.py:83
  74.5 7.3 %fusion.6 = (f32[28,4,160]{2,1,0:T(4,128)S(1)}, f32[28,4,160,160]{2,3,1,0:T(8,128)S(1)}) fusion(pred[28,160]{1,0:T(8,128)(4,1)S(1)} %iota_compare_fusion.1, bf16[28,160,4,64]{1,3,2,0:T(8,128)(2,1)} %copy.78, bf16[28,160,4,64]{1,3,2,0:T(8,128)(2,1)} %copy.79), kind=kOutput, calls=%fused_computation.22 | convolution fusion | flops 375585280 | bytes 16132480 | tf_op jit(solution)/shard_map/cqhd,ckhd->chqk/dot_general | solution.py:40
  88.1 8.0 %convert_bitcast_fusion = bf16[28,160,4,64]{1,3,2,0:T(8,128)(2,1)} fusion(bf16[28,160,4,64]{1,3,2,0:T(8,128)(2,1)} %copy.80, f32[28,4,160,160]{2,3,1,0:T(8,128)S(1)} %get-tuple-element.111, f32[28,4,160]{2,1,0:T(4,128)S(1)} %bitcast.72, pred[28,160]{1,0:T(8,128)(4,1)S(1)} %iota_compare_fusion.1), kind=kOutput, calls=%fused_computation.56 | convolution fusion | flops 379617280 | bytes 16132480 | tf_op jit(solution)/shard_map/chqk,ckhd->cqhd/dot_general | solution.py:90
  96.1 6.3 copy.82
  102.4 6.4 convert_element_type.190
  115.7 18.1 %reduce-scatter.5.cloned.1.call-done = f32[2240,512]{1,0:T(8,128)} async-done(((f32[4480,512]{1,0:T(8,128)}), f32[2240,512]{1,0:T(8,128)}) %reduce-scatter.5.cloned.1.call-update) | async-done | bytes 4587536 | tf_op jit(solution)/shard_map/reduce_scatter | solution.py:94
  141.9 15.7 %all-gather.7.cloned.1.call-done = bf16[4480,512]{1,0:T(8,128)(2,1)} async-done(((bf16[2240,512]{1,0:T(8,128)(2,1)}), bf16[4480,512]{1,0:T(8,128)(2,1)}) %all-gather.7.cloned.1.call-update) | async-done | bytes 4587536 | tf_op jit(solution)/shard_map/all_gather | solution.py:102
  157.6 46.7 %multiply_convert_fusion.1 = (bf16[4480,1024]{1,0:T(8,128)(2,1)S(1)}, f32[4480,1024]{1,0:T(8,128)}, f32[4480,1024]{1,0:T(8,128)}) fusion(f32[1024]{0:T(1024)S(1)} %convert_element_type.195, bf16[4480,512]{1,0:T(8,128)(2,1)} %all-gather.7.cloned.1.call-done, bf16[512,1024]{1,0:T(8,128)(2,1)S(1)} %copy-done), kind=kOutput, calls=%fused_computation.5 | convolution fusion | flops 5000396800 | bytes 51515392 | tf_op jit(solution)/shard_map/dot_general | solution.py:14
  207.9 7.5 %fusion.44 = f32[4480,512]{1,0:T(8,128)} fusion(bf16[4480,1024]{1,0:T(8,128)(2,1)S(1)} %get-tuple-element.105, bf16[1024,512]{1,0:T(8,128)(2,1)S(1)} %copy-done.44), kind=kOutput, calls=%fused_computation.109 | convolution fusion | flops 4697620480 | bytes 19398656 | tf_op jit(solution)/shard_map/dot_general | solution.py:14
  216.5 17.8 %reduce-scatter.7.cloned.1.call-done = f32[2240,512]{1,0:T(8,128)} async-done(((f32[4480,512]{1,0:T(8,128)}), f32[2240,512]{1,0:T(8,128)}) %reduce-scatter.7.cloned.1.call-update) | async-done | bytes 4587536 | tf_op jit(solution)/shard_map/reduce_scatter | solution.py:106
  252.9 15.7 %all-gather.9.cloned.1.call-done = bf16[4480,512]{1,0:T(8,128)(2,1)} async-done(((bf16[2240,512]{1,0:T(8,128)(2,1)}), bf16[4480,512]{1,0:T(8,128)(2,1)}) %all-gather.9.cloned.1.call-update) | async-done | bytes 4587536 | tf_op jit(solution)/shard_map/all_gather | solution.py:126
  268.6 20.0 %fusion.35 = (bf16[1024]{0:T(1024)(128)(2,1)S(1)}, bf16[4480,1024]{1,0:T(8,128)(2,1)}) fusion(f32[4480,1024]{1,0:T(8,128)} %get-tuple-element.106, f32[4480,1024]{1,0:T(8,128)} %get-tuple-element.112, f32[1024]{0:T(1024)S(1)} %convert_element_type.195, bf16[4480,512]{1,0:T(8,128)(2,1)} %all-gather.9.cloned.1.call-done, bf16[1024,512]{1,0:T(8,128)(2,1)S(1)} %copy-done.44), kind=kOutput, calls=%fused_computation.101 | convolution fusion | flops 4771019776 | bytes 51517440 | tf_op jit(solution)/shard_map/dot_general | solution.py:24
  288.6 11.1 %fusion.45 = f32[4480,512]{1,0:T(8,128)} fusion(bf16[4480,1024]{1,0:T(8,128)(2,1)} %get-tuple-element.97, bf16[512,1024]{1,0:T(8,128)(2,1)S(1)} %copy-done), kind=kOutput, calls=%fused_computation.110 | convolution fusion | flops 4697620480 | bytes 19398656 | tf_op jit(solution)/shard_map/dot_general | solution.py:24
  299.8 18.8 %reduce-scatter.9.cloned.1.call-done = f32[2240,512]{1,0:T(8,128)} async-done(((f32[4480,512]{1,0:T(8,128)}), f32[2240,512]{1,0:T(8,128)}) %reduce-scatter.9.cloned.1.call-update) | async-done | bytes 4587536 | tf_op jit(solution)/shard_map/reduce_scatter | solution.py:133
  333.1 9.9 %convolution_convert_fusion.3 = bf16[1024,512]{1,0:T(8,128)(2,1)} fusion(bf16[4480,1024]{1,0:T(8,128)(2,1)} %copy-done.45, bf16[4480,512]{1,0:T(8,128)(2,1)} %all-gather.9.cloned.1.call-done), kind=kOutput, calls=%fused_computation.58 | convolution fusion | flops 4698144768 | bytes 14811136 | tf_op jit(solution)/shard_map/dot_general | solution.py:18
  343.1 10.8 %convolution_convert_fusion.4 = bf16[512,1024]{1,0:T(8,128)(2,1)} fusion(bf16[4480,512]{1,0:T(8,128)(2,1)} %all-gather.7.cloned.1.call-done, bf16[4480,1024]{1,0:T(8,128)(2,1)} %get-tuple-element.97), kind=kOutput, calls=%fused_computation.59 | convolution fusion | flops 4698144768 | bytes 14811136 | tf_op jit(solution)/shard_map/dot_general | solution.py:18
  361.5 8.4 %copy.84 = bf16[28,160,4,64]{1,3,2,0:T(8,128)(2,1)} copy(bf16[28,160,4,64]{3,2,1,0:T(4,128)(2,1)} %reshape.191) | data formatting | bytes 4587520 | tf_op jit(solution)/shard_map/reshape | solution.py:142
  370.0 11.1 %fusion.42 = (bf16[4,64]{1,0:T(4,128)(2,1)S(1)}, bf16[28,4,64,160]{3,2,1,0:T(8,128)(2,1)}) fusion(bf16[28,160,4,64]{1,3,2,0:T(8,128)(2,1)} %copy.84, f32[28,4,160,160]{2,3,1,0:T(8,128)} %copy-done.1, f32[28,4,160]{2,1,0:T(4,128)S(1)} %bitcast.73, pred[28,160]{1,0:T(8,128)(4,1)S(1)} %copy-done.20), kind=kOutput, calls=%fused_computation.107 | convolution fusion | flops 380763904 | bytes 16132992 | tf_op jit(solution)/shard_map/chqk,cqhd->ckhd/dot_general | solution.py:159
  381.1 15.4 %multiply_reduce_fusion = (f32[28,4,160]{2,1,0:T(4,128)S(1)}, f32[28,4,160,160]{2,3,1,0:T(8,128)}) fusion(f32[28,4,160,160]{2,3,1,0:T(8,128)} %copy-done.1, f32[28,4,160]{2,1,0:T(4,128)S(1)} %bitcast.74, pred[28,160]{1,0:T(8,128)(4,1)S(1)} %copy-done.20, bf16[28,160,4,64]{1,3,2,0:T(8,128)(2,1)} %copy.84, bf16[28,160,4,64]{1,3,2,0:T(8,128)(2,1)} %copy.80), kind=kOutput, calls=%fused_computation.3 | convolution fusion | flops 381319680 | bytes 27672960 | tf_op jit(solution)/shard_map/cqhd,ckhd->chqk/dot_general | solution.py:145
  396.5 17.2 %multiply_convert_fusion = bf16[28,4,160,160]{2,3,1,0:T(8,128)(2,1)} fusion(f32[28,4,160,160]{2,3,1,0:T(8,128)} %get-tuple-element.114, f32[28,4,160,160]{2,3,1,0:T(8,128)} %copy-done.1, f32[28,4,160]{2,1,0:T(4,128)S(1)} %get-tuple-element.113, f32[28,4,160]{2,1,0:T(4,128)S(1)} %bitcast.75, pred[28,160]{1,0:T(8,128)(4,1)S(1)} %copy-done.20), kind=kLoop, calls=%fused_computation.2 | loop fusion | flops 17203200 | bytes 28819840 | tf_op jit(solution)/shard_map/convert_element_type | solution.py:149
  413.7 9.7 %fusion.13 = bf16[28,160,4,64]{1,3,2,0:T(8,128)(2,1)} fusion(bf16[28,160,4,64]{1,3,2,0:T(8,128)(2,1)} %copy.78, bf16[28,4,160,160]{2,3,1,0:T(8,128)(2,1)} %multiply_convert_fusion), kind=kOutput, calls=%fused_computation.55 | convolution fusion | flops 369295360 | bytes 10321920 | tf_op jit(solution)/shard_map/chqk,cqhd->ckhd/dot_general | solution.py:156
  423.5 8.1 %fusion.41 = (bf16[4,64]{1,0:T(4,128)(2,1)S(1)}, bf16[28,4,64,160]{3,2,1,0:T(8,128)(2,1)}) fusion(bf16[28,160,4,64]{1,3,2,0:T(8,128)(2,1)} %copy.79, bf16[28,4,160,160]{2,3,1,0:T(8,128)(2,1)} %multiply_convert_fusion), kind=kOutput, calls=%fused_computation.106 | convolution fusion | flops 370441984 | bytes 10322432 | tf_op jit(solution)/shard_map/chqk,ckhd->cqhd/dot_general | solution.py:152
  435.8 7.4 %convert_element_type.215 = bf16[4480,256]{0,1:T(8,128)(2,1)} reshape(bf16[28,160,4,64]{1,0,3,2:T(8,128)(2,1)} %copy.94) | data formatting | bytes 4587520 | tf_op jit(solution)/shard_map/convert_element_type | solution.py:165
  449.4 6.7 %convert_element_type.209 = bf16[4480,256]{0,1:T(8,128)(2,1)S(1)} reshape(bf16[28,160,4,64]{1,0,3,2:T(8,128)(2,1)} %copy.88) | data formatting | bytes 4587520 | tf_op jit(solution)/shard_map/convert_element_type | solution.py:163
  456.1 7.1 %copy.91 = bf16[28,160,4,64]{1,0,3,2:T(8,128)(2,1)} copy(bf16[28,160,4,64]{1,3,2,0:T(8,128)(2,1)} %fusion.13) | data formatting | bytes 4587520 | tf_op jit(solution)/shard_map/convert_element_type | solution.py:164
  463.1 7.4 %convert_element_type.212 = bf16[4480,256]{0,1:T(8,128)(2,1)} reshape(bf16[28,160,4,64]{1,0,3,2:T(8,128)(2,1)} %copy.91) | data formatting | bytes 4587520 | tf_op jit(solution)/shard_map/convert_element_type | solution.py:164
  496.1 42.5 %all-reduce = (f32[512]{0:T(512)}, f32[512]{0:T(512)}, f32[512]{0:T(512)}, f32[512]{0:T(512)}, f32[512]{0:T(512)}, /*index=5*/f32[512]{0:T(512)}) all-reduce(f32[512]{0:T(512)S(1)} %get-tuple-element.94, f32[512]{0:T(512)S(1)} %get-tuple-element.68, ...), channel_id=1, replica_groups=mesh['dp'=16,'tensor'=2] {'dp','tensor'}, use_global_device_ids=true, to_apply=%region_27.28 | all-reduce | flops 3072 | bytes 24576 | tf_op jit(solution)/shard_map/psum | solution.py:210
  538.8 41.3 %all-reduce.1 = (bf16[256]{0:T(256)(128)(2,1)S(1)}, bf16[256]{0:T(256)(128)(2,1)S(1)}, bf16[1024]{0:T(1024)(128)(2,1)S(1)}) all-reduce(bf16[256]{0:T(256)(128)(2,1)S(1)} %reduce_sum.257, bf16[256]{0:T(256)(128)(2,1)S(1)} %reduce_sum.259, bf16[1024]{0:T(1024)(128)(2,1)S(1)} %get-tuple-element.96), channel_id=1, replica_groups=mesh['dp'=16,'tensor'=2] {'dp'}, use_global_device_ids=true, to_apply=%region_20.21 | all-reduce | flops 1536 | bytes 6144 | tf_op jit(solution)/shard_map/psum | solution.py:194
  581.8 54.0 %all-reduce.5.cloned.1.call-done = (bf16[512,256]{0,1:T(8,128)(2,1)}, bf16[512,256]{0,1:T(8,128)(2,1)}, bf16[512,256]{0,1:T(8,128)(2,1)}, bf16[256,512]{1,0:T(8,...) async-done(((bf16[512,256]{0,1:T(8,128)(2,1)}, bf16[512,256]{0,1:T(8,128)(2,1)}, bf16[512,256]{0,1:T(8,128)(2,1)}, bf16[256,512]{1,0:T(8,128)(2,1)}, ...) | async-done | bytes 3145744 | tf_op jit(solution)/shard_map/psum | solution.py:193
  (181 shorter events, 149.7 us)
Async XLA Ops:
  7.2 150.4 %copy-start = (bf16[512,1024]{1,0:T(8,128)(2,1)S(1)}, bf16[512,1024]{1,0:T(8,128)(2,1)}, u32[]{:S(2)}) copy-start(bf16[512,1024]{1,0:T(8,128)(2,1)} %param.34) | copy-start | bytes 3145732
  7.2 19.4 %all-gather.5.cloned.1.call-start = ((), (), s32[]{:S(2)}) async-start(), calls=%async_computation.4 | async-start | bytes 6881280 | tf_op jit(solution)/shard_map/all_gather | solution.py:81
  7.9 125.9 %reduce-scatter.5.cloned.1.call-start = ((), (), s32[]{:S(2)}) async-start(), calls=%async_computation.5 | async-start | bytes 13762560 | tf_op jit(solution)/shard_map/reduce_scatter | solution.py:94
  10.0 77.2 %copy-start.19 = (pred[28,160]{1,0:T(8,128)(4,1)}, pred[28,160]{1,0:T(8,128)(4,1)S(1)}, u32[]{:S(2)}) copy-start(pred[28,160]{1,0:T(8,128)(4,1)S(1)} %iota_compare_fusion.1) | copy-start | bytes 13444
  81.8 6.3 copy-start.1
  87.2 8.9 %copy-start.15 = (f32[14,8,160]{2,1,0:T(8,128)}, f32[14,8,160]{2,1,0:T(8,128)S(1)}, u32[]{:S(2)}) copy-start(f32[14,8,160]{2,1,0:T(8,128)S(1)} %log_add_fusion) | copy-start | bytes 215044
  108.8 6.1 copy-start.9
  115.0 18.8 %copy-start.10 = (bf16[2240,512]{1,0:T(8,128)(2,1)S(1)}, bf16[2240,512]{1,0:T(8,128)(2,1)}, u32[]{:S(2)}) copy-start(bf16[2240,512]{1,0:T(8,128)(2,1)} %param.20) | copy-start | bytes 6881284
  115.0 42.6 %all-gather.7.cloned.1.call-start = ((), (), s32[]{:S(2)}) async-start(), calls=%async_computation.6 | async-start | bytes 6881280 | tf_op jit(solution)/shard_map/all_gather | solution.py:102
  115.6 23.2 %copy-start.27 = (f32[512]{0:T(512)}, f32[512]{0:T(512)S(1)}, u32[]{:S(2)}) copy-start(f32[512]{0:T(512)S(1)} %convert_element_type.192) | copy-start | bytes 6148
  115.7 23.2 %copy-start.29 = (f32[512]{0:T(512)}, f32[512]{0:T(512)S(1)}, u32[]{:S(2)}) copy-start(f32[512]{0:T(512)S(1)} %convert_element_type.193) | copy-start | bytes 6148
  141.9 92.4 %reduce-scatter.7.cloned.1.call-start = ((), (), s32[]{:S(2)}) async-start(), calls=%async_computation.7 | async-start | bytes 13762560 | tf_op jit(solution)/shard_map/reduce_scatter | solution.py:106
  141.9 66.0 %copy-start.44 = (bf16[1024,512]{1,0:T(8,128)(2,1)S(1)}, bf16[1024,512]{1,0:T(8,128)(2,1)}, u32[]{:S(2)}) copy-start(bf16[1024,512]{1,0:T(8,128)(2,1)} %param.36) | copy-start | bytes 3145732
  204.4 3.6 copy-start.45
  215.4 18.8 %copy-start.18 = (f32[2240]{0:T(1024)S(1)}, f32[2240]{0:T(1024)}, u32[]{:S(2)}) copy-start(f32[2240]{0:T(1024)} %copy-done.17) | copy-start | bytes 26884
  215.5 18.8 %copy-start.22 = (f32[2240]{0:T(1024)S(1)}, f32[2240]{0:T(1024)}, u32[]{:S(2)}) copy-start(f32[2240]{0:T(1024)} %copy-done.21) | copy-start | bytes 26884
  215.5 18.8 %copy-start.28 = (f32[512]{0:T(512)S(1)}, f32[512]{0:T(512)}, u32[]{:S(2)}) copy-start(f32[512]{0:T(512)} %copy-done.27) | copy-start | bytes 6148
  215.5 18.8 %copy-start.30 = (f32[512]{0:T(512)S(1)}, f32[512]{0:T(512)}, u32[]{:S(2)}) copy-start(f32[512]{0:T(512)} %copy-done.29) | copy-start | bytes 6148
  215.5 53.1 %all-gather.9.cloned.1.call-start = ((), (), s32[]{:S(2)}) async-start(), calls=%async_computation.8 | async-start | bytes 6881280 | tf_op jit(solution)/shard_map/all_gather | solution.py:126
  252.8 65.7 %reduce-scatter.9.cloned.1.call-start = ((), (), s32[]{:S(2)}) async-start(), calls=%async_computation.9 | async-start | bytes 13762560 | tf_op jit(solution)/shard_map/reduce_scatter | solution.py:133
  299.7 25.0 %copy-start.26 = (f32[2240]{0:T(1024)S(1)}, f32[2240]{0:T(1024)}, u32[]{:S(2)}) copy-start(f32[2240]{0:T(1024)} %copy-done.25) | copy-start | bytes 26884
  299.7 54.2 %all-gather.11.cloned.1.call-start = ((), (), s32[]{:S(2)}) async-start(), calls=%async_computation.10 | async-start | bytes 6881280 | tf_op jit(solution)/shard_map/all_gather | solution.py:139
  333.1 302.6 %all-reduce.5.cloned.1.call-start = ((), (), s32[]{:S(2)}) async-start(), calls=%async_computation.12 | async-start | bytes 6291456 | tf_op jit(solution)/shard_map/psum | solution.py:193
  361.5 8.4 %copy-start.16 = (f32[14,8,160]{2,1,0:T(8,128)S(1)}, f32[14,8,160]{2,1,0:T(8,128)}, u32[]{:S(2)}) copy-start(f32[14,8,160]{2,1,0:T(8,128)} %copy-done.15) | copy-start | bytes 215044
  361.5 8.4 %copy-start.20 = (pred[28,160]{1,0:T(8,128)(4,1)S(1)}, pred[28,160]{1,0:T(8,128)(4,1)}, u32[]{:S(2)}) copy-start(pred[28,160]{1,0:T(8,128)(4,1)} %copy-done.19) | copy-start | bytes 13444
  423.5 8.1 %copy-start.13 = (bf16[28,4,64,160]{3,2,1,0:T(8,128)(2,1)S(1)}, bf16[28,4,64,160]{3,2,1,0:T(8,128)(2,1)}, u32[]{:S(2)}) copy-start(bf16[28,4,64,160]{3,2,1,0:T(8,128)(2,1)} %get-tuple-element.118) | copy-start | bytes 6881284
  456.1 24.2 %copy-start.5 = (bf16[4480,256]{0,1:T(8,128)(2,1)}, bf16[4480,256]{0,1:T(8,128)(2,1)S(1)}, u32[]{:S(2)}) copy-start(bf16[4480,256]{0,1:T(8,128)(2,1)S(1)} %convert_element_type.209) | copy-start | bytes 6881284
  470.5 5.2 copy-start.11
  470.5 9.7 %slice-start = ((s8[4587520]{0:T(1024)(128)(4,1)}), s8[4194304]{0:T(1024)(128)(4,1)S(1)}, s32[]{:S(2)}) async-start(s8[4587520]{0:T(1024)(128)(4,1)} %bitcast.77), calls=%async_computation.13 | async-start | bytes 8388608
  475.7 4.5 slice-start.1
  484.5 165.7 %reduce-scatter.11.cloned.1.call-start = ((), (), s32[]{:S(2)}) async-start(), calls=%async_computation.11 | async-start | bytes 6881280 | tf_op jit(solution)/shard_map/reduce_scatter | solution.py:177
  635.7 10.4 %copy-start.14 = (bf16[1024,512]{1,0:T(8,128)(2,1)S(1)}, bf16[1024,512]{1,0:T(8,128)(2,1)}, u32[]{:S(2)}) copy-start(bf16[1024,512]{1,0:T(8,128)(2,1)} %get-tuple-element.91) | copy-start | bytes 3145732
  (25 other events, 32.8 us)
Sparse Core Ops, SparseCore 0:
  9.6 16.9 all-gather.4
  115.1 18.6 reduce-scatter.4
  142.0 15.6 all-gather.6
  215.6 18.6 reduce-scatter.6
  253.0 15.6 all-gather.8
  299.8 18.6 reduce-scatter.8
  333.2 15.5 all-gather.10
  484.6 151.1 all-reduce.4
  638.7 11.3 reduce-scatter.10
where the time goes:
time: 673 us; the launch traced here: 663 us
  matrix products  210 us (31%)
  waiting for transfers between devices  160 us (24%)
  local copies, waits for them, and re-layouts  121 us (18%)
  blocking collectives  83.7 us (12%)
  other arithmetic  72.9 us (11%)
  between operations  14.8 us (2%)
    dot_general x6, matrix products, product(): return jnp.dot(left, right, preferred_element_type=jnp.float32)  71.4 us
    psum x1, waiting for transfers between devices, local(): lax.psum(query_weight_part.astype(jnp.bfloat16), 'dp').astype(jnp.float32)  54 us
    dot_general x6, matrix products, product_right(): lax.dot_general(left, right, (((1,), (1,)), ((), ())), preferred_element_...  44.1 us
    psum x1, blocking collectives, local(): lax.psum((output_bias_part, first_gain_part, first_shift_part, down_bias_...  42.5 us
    psum x1, blocking collectives, local(): lax.psum(query_bias_part.astype(jnp.bfloat16), 'dp').astype(jnp.float32)  41.3 us
    dot_general x6, matrix products, product_left(): lax.dot_general(left, right, (((0,), (0,)), ((), ())), preferred_element_...  34.7 us
    unnamed x99, local copies, waits for them, and re-layouts  20.4 us
    reduce_scatter x1, waiting for transfers between devices, local(): lax.psum_scatter(product_right(grad_hidden_low, inner_weight), 'tensor',...  18.8 us
  transfers between devices with their start and end apart: 9, of which 8 were waited for; matrix products, arithmetic and copies ran while one was open for 7% of the time, Pallas kernels for 0%

commit v1 on v0

--- a/solution.py
+++ b/solution.py
@@ -1,12 +1,17 @@
+import functools
+
 import jax
 import jax.numpy as jnp
 from jax import lax
+from jax.experimental import pallas as pl
+from jax.experimental.pallas import tpu as pltpu
 from jax.sharding import PartitionSpec as P
 
+MESH = pl.DeviceIdType.MESH
+f32, bf16 = jnp.float32, jnp.bfloat16
 HEAD_DIM = 64
 SEQ = 160
-
-
+ROWS = 3072
 EPSILON = 1e-12
 
 
@@ -51,7 +56,7 @@
     return jnp.sum(values.astype(jnp.float32), axis=0)
 
 
-def local(
+def general(
     states,
     cotangent,
     lengths,
@@ -239,6 +244,243 @@
     )
 
 
+class Comm:
+    NSTAGE = 10
+    def __init__(self, K, g, small, out, sout, bufs, stride=1):
+        self.stride = stride
+        self.K = K; self.CH = ROWS // K; self.SB = self.CH // 3
+        self.g, self.small, self.out, self.sout = g, small, out, sout
+        (self.core_buf, self.acc, self.r1, self.r2, self.r3, self.r4, self.sm, self.csem, self.rsem, self.asem, self.smsem) = bufs
+        dp = lax.axis_index("dp"); t = lax.axis_index("tensor")
+        self.t = t
+        x = lax.rem(dp, 2); y = lax.rem(dp // 2, 2); p = lax.rem(dp // 4, 2); q = dp // 8
+        self.bits = (x, y, p, q)
+        self.parts = tuple(dp + w * (1 - 2 * b) for w, b in ((1, x), (2, y), (4, p), (8, q)))
+        self.dp = dp
+    def barrier(self):
+        b = pltpu.get_barrier_semaphore()
+        pl.semaphore_signal(b, inc=1, device_id=(self.dp, 1 - self.t), device_id_type=MESH)
+        for n in self.parts:
+            pl.semaphore_signal(b, inc=1, device_id=(n, self.t), device_id_type=MESH)
+        pl.semaphore_wait(b, 5)
+    def rc(self, src, dst, s, r, n):
+        return pltpu.make_async_remote_copy(src_ref=src, dst_ref=dst, send_sem=s, recv_sem=r, device_id=(n, self.t), device_id_type=MESH)
+    def core_copy(self, k):
+        return pltpu.make_async_remote_copy(src_ref=self.g.at[1 - self.t, pl.ds(k * self.CH, self.CH)], dst_ref=self.core_buf.at[k],
+            send_sem=self.csem.at[0, k], recv_sem=self.csem.at[1, k], device_id=(self.dp, 1 - self.t), device_id_type=MESH)
+    def order(self, k, r):
+        B, N = self.bits, self.parts
+        X, Y, Pp, Qq = ((B[i], N[i]) for i in range(4))
+        if r == 0: return X, Y, Pp, Qq
+        if r == 1: return Y, X, Pp, Qq
+        even = lax.rem(k, 2) == 0
+        U = (jnp.where(even, B[0], B[1]), jnp.where(even, N[0], N[1]))
+        V = (jnp.where(even, B[1], B[0]), jnp.where(even, N[1], N[0]))
+        return Pp, U, V, Qq
+    def region(self, k, r, depth, keep):
+        o = self.order(k, r)
+        rows, cols = self.SB, 512
+        r0, c0 = k * self.CH + r * self.SB, 0
+        for i in range(depth):
+            b = o[i][0]
+            if i == depth - 1 and not keep: b = 1 - b
+            if i < 2:
+                rows //= 2; r0 = r0 + b * rows
+            else:
+                cols //= 2; c0 = c0 + b * cols
+        if depth > 2: c0 = pl.multiple_of(c0, 128)
+        return pl.ds(pl.multiple_of(r0, 16), rows), pl.ds(c0, cols)
+    def rs(self, k, r, i):
+        n = self.order(k, r)[i][1]
+        buf = (self.r1, self.r2, self.r3, self.r4)[i]
+        return self.rc(self.acc.at[self.region(k, r, i + 1, False)], buf.at[k, r], self.rsem.at[0, i, k, r], self.rsem.at[1, i, k, r], n)
+    def ag(self, k, r, i):
+        n = self.order(k, r)[i][1]
+        sl = self.region(k, r, i + 1, True)
+        return self.rc(self.out.at[sl], self.out.at[sl], self.asem.at[0, i, k, r], self.asem.at[1, i, k, r], n)
+    def small_copy(self, i):
+        dev = (self.dp, 1 - self.t) if i == 0 else (self.parts[i - 1], self.t)
+        src = self.small if i == 0 else self.sm.at[1, i - 1]
+        return pltpu.make_async_remote_copy(src_ref=src, dst_ref=self.sm.at[0, i], send_sem=self.smsem.at[0, i], recv_sem=self.smsem.at[1, i], device_id=dev, device_id_type=MESH)
+    def stage(self, s, k):
+        if s == 0:
+            self.core_copy(k).start()
+        elif s == 1:
+            self.core_copy(k).wait_recv()
+            sl = pl.ds(pl.multiple_of(k * self.CH, 16), self.CH)
+            self.acc[sl] = (self.g[self.t, sl].astype(f32) + self.core_buf[k].astype(f32)).astype(bf16)
+            for r in range(3): self.rs(k, r, 0).start()
+        elif s <= 5:
+            i = s - 2
+            buf = (self.r1, self.r2, self.r3, self.r4)[i]
+            for r in range(3):
+                self.rs(k, r, i).wait_recv()
+                sl = self.region(k, r, i + 1, True)
+                v = (self.acc[sl].astype(f32) + buf[k, r].astype(f32)).astype(bf16)
+                if i < 3:
+                    self.acc[sl] = v
+                    self.rs(k, r, i + 1).start()
+                else:
+                    self.out[sl] = v
+                    self.ag(k, r, 3).start()
+        else:
+            i = 9 - s
+            for r in range(3):
+                self.ag(k, r, i).wait_recv()
+                if i > 0: self.ag(k, r, i - 1).start()
+    def small_stage(self, i):
+        if i > 0:
+            self.small_copy(i - 1).wait_recv()
+            own = self.small[...] if i == 1 else self.sm[1, i - 2]
+            v = own + self.sm[0, i - 1]
+            if i < 5: self.sm[1, i - 1] = v
+            else: self.sout[...] = v
+        if i < 5: self.small_copy(i).start()
+    def iteration(self, it):
+        for s in reversed(range(self.NSTAGE)):
+            k = it - s * self.stride
+            @pl.when((k >= 0) & (k < self.K))
+            def _(s=s, k=k):
+                self.stage(s, k)
+        for i in range(6):
+            @pl.when(it == i * self.stride + 1)
+            def _(i=i): self.small_stage(i)
+    @property
+    def iterations(self): return self.K + (self.NSTAGE - 1) * self.stride
+    def finish(self):
+        def body(k, c):
+            self.core_copy(k).wait_send()
+            for r in range(3):
+                for i in range(4):
+                    self.rs(k, r, i).wait_send(); self.ag(k, r, i).wait_send()
+            return c
+        lax.fori_loop(0, self.K, body, 0)
+        for i in range(5): self.small_copy(i).wait_send()
+    @staticmethod
+    def scratch(K, S):
+        SB = ROWS // K // 3
+        D = pltpu.SemaphoreType.DMA
+        return [pltpu.VMEM((K, 3 * SB, 512), bf16), pltpu.VMEM((ROWS, 512), bf16),
+            pltpu.VMEM((K, 3, SB // 2, 512), bf16), pltpu.VMEM((K, 3, SB // 4, 512), bf16),
+            pltpu.VMEM((K, 3, SB // 4, 256), bf16), pltpu.VMEM((K, 3, SB // 4, 128), bf16),
+            pltpu.VMEM((2, 5, S, 512), f32),
+            D((2, K)), D((2, 4, K, 3)), D((2, 4, K, 3)), D((2, 5))]
+
+def kern(K, stride, g, small, out, sout, *bufs):
+    c = Comm(K, g, small, out, sout, bufs, stride)
+    c.barrier()
+    def body(it, _):
+        c.iteration(it); return _
+    lax.fori_loop(0, c.iterations, body, 0)
+    c.finish()
+
+def comm(g, small, K=8, stride=1):
+    S = small.shape[0]
+    V = pl.BlockSpec(memory_space=pltpu.VMEM)
+    return pl.pallas_call(functools.partial(kern, K, stride),
+        out_shape=(jax.ShapeDtypeStruct((ROWS, 512), bf16), jax.ShapeDtypeStruct((S, 512), f32)),
+        in_specs=[V, V], out_specs=(V, V), scratch_shapes=Comm.scratch(K, S),
+        compiler_params=pltpu.CompilerParams(collective_id=0, has_side_effects=True, vmem_limit_bytes=50 << 20), name="comm")(g, small)
+
+
+def pack_half(dq, dk, dv, do, di, dd):
+    vo = jnp.concatenate([dv, jnp.concatenate([do[:, :256], do[:, 256:]], axis=0)], axis=1)
+    return jnp.concatenate([dd, di[:, :512], di[:, 512:], jnp.concatenate([dq, dk], axis=1), vo], axis=0)
+
+
+def unpack_half(w):
+    do = w[2560:3072, 256:]
+    return dict(
+        down=w[:1024], inner=jnp.concatenate([w[1024:1536], w[1536:2048]], axis=1),
+        query=w[2048:2560, :256], key=w[2048:2560, 256:], value=w[2560:3072, :256],
+        output=jnp.concatenate([do[:256], do[256:]], axis=1),
+    )
+
+
+def whole_chains(
+    states, cotangent, lengths, span_starts, span_ends, query_weight, query_bias, key_weight, value_weight, value_bias,
+    output_weight, output_bias, first_gain, first_shift, inner_weight, inner_bias, down_weight, down_bias, second_gain, second_shift,
+):
+    t = lax.axis_index("tensor")
+    gather = lambda a, axis: lax.all_gather(a, "tensor", axis=axis, tiled=True)
+    wq, wk, wv = gather(query_weight, 1), gather(key_weight, 1), gather(value_weight, 1)
+    wo, wi, wd = gather(output_weight, 0), gather(inner_weight, 1), gather(down_weight, 0)
+    bq, bv, bi = gather(query_bias, 0), gather(value_bias, 0), gather(inner_bias, 0)
+    rows = states.shape[0]
+    chains = rows // SEQ
+    heads = wq.shape[1] // HEAD_DIM
+    mine = lambda a: lax.dynamic_slice_in_dim(a, t * chains, chains)
+    lengths, span_starts, span_ends = mine(lengths), mine(span_starts), mine(span_ends)
+    layout = (chains, SEQ, heads, HEAD_DIM)
+    queries = (product(states, wq) + bq).astype(bf16).reshape(layout)
+    keys = product(states, wk).astype(bf16).reshape(layout)
+    values = (product(states, wv) + bv).astype(bf16).reshape(layout)
+    key_live = jnp.arange(SEQ, dtype=jnp.int32)[None, :] < lengths[:, None]
+    scores = attention_scores(queries, keys, key_live)
+    highest = jnp.max(scores, axis=-1, keepdims=True)
+    logsum = highest + jnp.log(jnp.sum(jnp.exp(scores - highest), axis=-1, keepdims=True))
+    probs = jnp.exp(scores - logsum)
+    probs_low = probs.astype(bf16)
+    context = jnp.einsum("chqk,ckhd->cqhd", probs_low, values, preferred_element_type=f32)
+    context = context.reshape(rows, heads * HEAD_DIM).astype(bf16)
+    first_sum = states.astype(f32) + product(context, wo) + output_bias.astype(f32)
+    normed, first_pull = jax.vjp(layer_norm, first_sum, first_gain.astype(f32), first_shift.astype(f32))
+    normed_low = normed.astype(bf16)
+    hidden = product(normed_low, wi) + bi.astype(f32)
+    activation, gelu_pull = jax.vjp(exact_gelu, hidden)
+    activation_low = activation.astype(bf16)
+    second_sum = normed + product(activation_low, wd) + down_bias.astype(f32)
+    output, second_pull = jax.vjp(layer_norm, second_sum, second_gain.astype(f32), second_shift.astype(f32))
+    position = jnp.arange(SEQ, dtype=jnp.int32)[None, :]
+    live = (position >= span_starts[:, None]) & (position < span_ends[:, None]) & key_live
+    grad_out = jnp.where(live.reshape(rows, 1), cotangent.astype(f32), 0.0)
+    grad_second, second_gain_part, second_shift_part = second_pull(grad_out)
+    grad_branch = grad_second.astype(bf16)
+    down_weight_part = product_left(activation_low, grad_branch)
+    (grad_hidden,) = gelu_pull(product_right(grad_branch, wd))
+    grad_hidden = grad_hidden.astype(bf16)
+    inner_weight_part = product_left(normed_low, grad_hidden)
+    grad_normed = product_right(grad_hidden, wi) + grad_second
+    grad_first, first_gain_part, first_shift_part = first_pull(grad_normed)
+    grad_attended = grad_first.astype(bf16)
+    output_weight_part = product_left(context, grad_attended)
+    grad_context = product_right(grad_attended, wo).astype(bf16).reshape(layout)
+    grad_probs = jnp.einsum("cqhd,ckhd->chqk", grad_context, values, preferred_element_type=f32)
+    grad_scores = (probs * (grad_probs - jnp.sum(probs * grad_probs, axis=-1, keepdims=True))).astype(bf16)
+    scale = HEAD_DIM ** (-0.5)
+    flat = (rows, heads * HEAD_DIM)
+    grad_queries = (jnp.einsum("chqk,ckhd->cqhd", grad_scores, keys, preferred_element_type=f32) * scale).reshape(flat).astype(bf16)
+    grad_keys = (jnp.einsum("chqk,cqhd->ckhd", grad_scores, queries, preferred_element_type=f32) * scale).reshape(flat).astype(bf16)
+    grad_values = jnp.einsum("chqk,cqhd->ckhd", probs_low, grad_context, preferred_element_type=f32).reshape(flat).astype(bf16)
+    query_weight_part = product_left(states, grad_queries)
+    key_weight_part = product_left(states, grad_keys)
+    value_weight_part = product_left(states, grad_values)
+    input_grad = product_right(grad_queries, wq) + product_right(grad_keys, wk) + product_right(grad_values, wv) + grad_first
+    halves = jnp.stack([
+        pack_half(query_weight_part[:, a * 256:a * 256 + 256], key_weight_part[:, a * 256:a * 256 + 256],
+                  value_weight_part[:, a * 256:a * 256 + 256], output_weight_part[a * 256:a * 256 + 256],
+                  inner_weight_part[:, a * 1024:a * 1024 + 1024], down_weight_part[a * 1024:a * 1024 + 1024])
+        for a in (0, 1)]).astype(bf16)
+    small = jnp.stack([
+        column_sum(grad_attended), first_gain_part, first_shift_part, column_sum(grad_branch), second_gain_part, second_shift_part,
+        column_sum(grad_queries), column_sum(grad_values), *column_sum(grad_hidden).reshape(4, 512)] + [jnp.zeros((512,), f32)] * 4)
+    summed, small = comm(halves, small, 4, 2)
+    w = {k: v.astype(f32) for k, v in unpack_half(summed).items()}
+    half = lambda row: lax.dynamic_slice_in_dim(row, t * 256, 256)
+    return (
+        output.astype(bf16), input_grad, w["query"], half(small[6]), w["key"], w["value"], half(small[7]), w["output"],
+        small[0], small[1], small[2], w["inner"], lax.dynamic_slice_in_dim(small[8:12].reshape(2048), t * 1024, 1024),
+        w["down"], small[3], small[4], small[5],
+    )
+
+
+def local(*arguments):
+    rows, hidden = arguments[0].shape[0], arguments[14].shape[1]
+    if rows % SEQ == 0 and lax.axis_size("dp") == 16 and lax.axis_size("tensor") == 2:
+        return whole_chains(*arguments)
+    return general(*arguments)
+
+
 def solution(mesh):
     placed = (
         P(("dp", "tensor"), None),

time: 673 us -> 503 us (0.75)
  waiting for transfers between devices: 160 us -> 1.38 us
  Pallas kernels: 0 us -> 70.4 us
  blocking collectives: 83.7 us -> 14.8 us
  other arithmetic: 72.9 us -> 60.6 us
    psum x2 -> x0, blocking collectives: 83.7 us -> none  [the longest x1 42.5 us: local(): lax.psum((output_bias_part, first_gain_part, first_shift_part, down_bias_...]
    pallas_call x0 -> x1, Pallas kernels: none -> 70.4 us  [comm(): pl.pallas_call(functools.partial(kern, K, stride), out_shape=(jax.ShapeDt...]
    reduce_scatter x4 -> x0, waiting for transfers between devices: 57.1 us -> none  [the longest x1 18.8 us: local(): lax.psum_scatter(product_right(grad_hidden_low, inner_weight), 'tensor',...]
    psum x1 -> x0, waiting for transfers between devices: 54 us -> none  [local(): lax.psum(query_weight_part.astype(jnp.bfloat16), 'dp').astype(jnp.float32)]
    all_gather x4 -> x2, waiting for transfers between devices: 47.9 us -> 0.01 us  [whole_chains(): gather = lambda a, axis: lax.all_gather(a, 'tensor', axis=axis, tiled=True)]
    all_gather x0 -> x7, blocking collectives: none -> 14.8 us  [whole_chains(): gather = lambda a, axis: lax.all_gather(a, 'tensor', axis=axis, tiled=True)]
    reduce_sum x4 -> x2, other arithmetic: 16.6 us -> 8.83 us  [layer_norm(): center = values - jnp.mean(values, axis=-1, keepdims=True)]
    dot_general x1, matrix products: 7.31 us -> 14.1 us  [attention_scores(): jnp.einsum('cqhd,ckhd->chqk', queries, keys, preferred_element_type=jnp.f...]
  transfers between devices with their start and end apart: 9 -> 2, of which waited for: 8 -> 0; matrix products, arithmetic and copies ran while one was open for 7% -> 29% of each run, Pallas kernels for 0% -> 0%
where the time goes in v1:
time: 503 us; the launch traced here: 496 us
  matrix products  210 us (42%)
  local copies, waits for them, and re-layouts  125 us (25%)
  Pallas kernels  70.4 us (14%)
  other arithmetic  60.6 us (12%)
  between operations  14.9 us (3%)
  blocking collectives  14.8 us (3%)
    dot_general x6, matrix products, product(): return jnp.dot(left, right, preferred_element_type=jnp.float32)  72.6 us
    pallas_call x1, Pallas kernels, comm(): pl.pallas_call(functools.partial(kern, K, stride), out_shape=(jax.ShapeDt...  70.4 us
    dot_general x6, matrix products, product_right(): lax.dot_general(left, right, (((1,), (1,)), ((), ())), preferred_element_...  45.2 us
    dot_general x6, matrix products, product_left(): lax.dot_general(left, right, (((0,), (0,)), ((), ())), preferred_element_...  29.4 us
    unnamed x119, local copies, waits for them, and re-layouts  22.9 us
    dot_general x1, matrix products, whole_chains(): jnp.einsum('cqhd,ckhd->chqk', grad_context, values, preferred_element_typ...  15.4 us
    all_gather x7, blocking collectives, whole_chains(): gather = lambda a, axis: lax.all_gather(a, 'tensor', axis=axis, tiled=True)  14.8 us
    convert_element_type x1, other arithmetic, whole_chains(): (probs * (grad_probs - jnp.sum(probs * grad_probs, axis=-1, keepdims=True...  14.5 us
  transfers between devices with their start and end apart: 2, of which 0 were waited for; matrix products, arithmetic and copies ran while one was open for 29% of the time, Pallas kernels for 0%

profile of v1, /device:TPU:0, one launch (start us, length us, event | category | flops | bytes accessed | tf_op | source)
XLA Modules:
  0.0 496.3 jit_solution(5060131636448446974)
XLA Ops:
  24.9 7.3 %copy.80 = bf16[14,160,8,64]{1,3,2,0:T(8,128)(2,1)} copy(bf16[14,160,8,64]{3,2,1,0:T(8,128)(2,1)} %reshape.236) | data formatting | bytes 4587520 | tf_op jit(solution)/shard_map/reshape | solution.py:417
  43.9 7.3 %copy.78 = bf16[14,160,8,64]{1,3,2,0:T(8,128)(2,1)} copy(bf16[14,160,8,64]{3,2,1,0:T(8,128)(2,1)} %reshape.237) | data formatting | bytes 4587520 | tf_op jit(solution)/shard_map/reshape | solution.py:415
  57.2 4.4 reshape.238
  61.6 7.3 %copy.79 = bf16[14,160,8,64]{1,3,2,0:T(8,128)(2,1)} copy(bf16[14,160,8,64]{3,2,1,0:T(8,128)(2,1)} %reshape.238) | data formatting | bytes 4587520 | tf_op jit(solution)/shard_map/reshape | solution.py:416
  68.9 14.1 %fusion.6 = (f32[14,8,160]{2,1,0:T(8,128)S(1)}, f32[14,8,160,160]{2,3,1,0:T(8,128)}) fusion(pred[14,160]{1,0:T(8,128)(4,1)S(1)} %get-tuple-element.74, bf16[14,160,8,64]{1,3,2,0:T(8,128)(2,1)} %copy.78, bf16[14,160,8,64]{1,3,2,0:T(8,128)(2,1)} %copy.79), kind=kOutput, calls=%fused_computation.23 | convolution fusion | flops 375585280 | bytes 16130240 | tf_op jit(solution)/shard_map/cqhd,ckhd->chqk/dot_general | solution.py:45
  83.0 10.5 %exponential_reduce_fusion = f32[14,8,160]{2,1,0:T(8,128)S(1)} fusion(f32[14,8,160,160]{2,3,1,0:T(8,128)} %get-tuple-element.76, f32[14,8,160]{2,1,0:T(8,128)S(1)} %get-tuple-element.75, pred[14,160]{1,0:T(8,128)(4,1)S(1)} %get-tuple-element.74), kind=kLoop, calls=%fused_computation.20 | loop fusion | flops 11450880 | bytes 11614400 | tf_op jit(solution)/shard_map/reduce_sum | solution.py:421
  93.6 8.6 %convert_bitcast_fusion = bf16[14,160,8,64]{1,3,2,0:T(8,128)(2,1)S(1)} fusion(bf16[14,160,8,64]{1,3,2,0:T(8,128)(2,1)S(1)} %copy-done.6, f32[14,8,160,160]{2,3,1,0:T(8,128)} %get-tuple-element.76, f32[14,8,160]{2,1,0:T(8,128)S(1)} %log_add_fusion, pred[14,160]{1,0:T(8,128)(4,1)S(1)} %get-tuple-element.74), kind=kOutput, calls=%fused_computation.63 | convolution fusion | flops 379617280 | bytes 16130240 | tf_op jit(solution)/shard_map/chqk,ckhd->cqhd/dot_general | solution.py:424
  102.2 4.4 copy.82
  106.6 6.9 %convert_element_type.156 = bf16[2240,512]{0,1:T(8,128)(2,1)S(1)} reshape(bf16[14,160,8,64]{1,0,3,2:T(8,128)(2,1)} %copy.82) | data formatting | bytes 4587520 | tf_op jit(solution)/shard_map/convert_element_type | solution.py:425
  124.7 48.2 %multiply_convert_fusion.1 = (bf16[2240,2048]{1,0:T(8,128)(2,1)}, f32[2240,2048]{1,0:T(8,128)}, f32[2240,2048]{1,0:T(8,128)}) fusion(f32[2048]{0:T(1024)S(1)} %convert_element_type.161, bf16[512,2048]{1,0:T(8,128)(2,1)} %all-gather.5.cloned.1.call-done, f32[2240,512]{1,0:T(8,128)} %copy-done.4, f32[512]{0:T(512)S(1)} %convert_element_type.159, ...), kind=kOutput, calls=%fused_computation.6 | convolution fusion | flops 5006131200 | bytes 52590080 | tf_op jit(solution)/shard_map/dot_general | solution.py:19
  172.9 11.7 %fusion.49 = (f32[2240]{0:T(1024)S(1)}, f32[2240,512]{1,0:T(8,128)S(1)}) fusion(f32[512]{0:T(512)S(1)} %copy-done.39, bf16[2240,2048]{1,0:T(8,128)(2,1)} %get-tuple-element.35, bf16[2048,512]{1,0:T(8,128)(2,1)} %all-gather.7.cloned.1.call-done, f32[512]{0:T(512)S(1)} %convert_element_type.159, f32[512]{0:T(512)S(1)} %convert_element_type.158, ...), kind=kOutput, calls=%fused_computation.129 | convolution fusion | flops 4705646592 | bytes 20480256 | tf_op jit(solution)/shard_map/dot_general | solution.py:19
  189.6 4.4 fusion.38
  197.2 20.7 %convert_reduce_fusion = (f32[2048]{0:T(1024)S(1)}, bf16[2240,2048]{1,0:T(8,128)(2,1)}) fusion(f32[2240,2048]{1,0:T(8,128)} %get-tuple-element.36, bf16[2240,512]{1,0:T(8,128)(2,1)S(1)} %get-tuple-element.28, bf16[2048,512]{1,0:T(8,128)(2,1)} %all-gather.7.cloned.1.call-done, f32[2240,2048]{1,0:T(8,128)} %get-tuple-element.79, ...), kind=kOutput, calls=%fused_computation.2 | convolution fusion | flops 4775606272 | bytes 50282496 | tf_op jit(solution)/shard_map/dot_general | solution.py:29
  217.9 11.9 %multiply_reduce_fusion.2 = (f32[512]{0:T(512)S(1)}, f32[2240]{0:T(1024)S(1)}, f32[512]{0:T(512)S(1)}, f32[2240,512]{1,0:T(8,128)S(1)}) fusion(f32[2240,512]{1,0:T(8,128)} %copy-done.4, f32[2240]{0:T(1024)S(1)} %fusion.28, f32[2240]{0:T(1024)S(1)} %broadcast_multiply_fusion.1, f32[512]{0:T(512)S(1)} %convert_element_type.158, f32[2240,512]{1,0:T(8,128)} %copy-done.5, ...), kind=kOutput, calls=%fused_computation.44 | convolution fusion | flops 4709086208 | bytes 25076736 | tf_op jit(solution)/shard_map/dot_general | solution.py:29
  229.8 4.4 fusion.37
  241.0 6.9 %reshape.239 = bf16[14,160,8,64]{3,2,1,0:T(8,128)(2,1)} reshape(bf16[2240,512]{1,0:T(8,128)(2,1)} %convolution_convert_fusion) | data formatting | bytes 4587520 | tf_op jit(solution)/shard_map/reshape | solution.py:447
  247.9 7.5 %copy.84 = bf16[14,160,8,64]{1,3,2,0:T(8,128)(2,1)} copy(bf16[14,160,8,64]{3,2,1,0:T(8,128)(2,1)} %reshape.239) | data formatting | bytes 4587520 | tf_op jit(solution)/shard_map/reshape | solution.py:447
  255.3 15.4 %multiply_reduce_fusion = (f32[14,8,160]{2,1,0:T(8,128)S(1)}, f32[14,8,160,160]{2,3,1,0:T(8,128)}) fusion(f32[14,8,160,160]{2,3,1,0:T(8,128)} %get-tuple-element.76, f32[14,8,160]{2,1,0:T(8,128)S(1)} %copy-done.22, pred[14,160]{1,0:T(8,128)(4,1)S(1)} %copy-done.32, bf16[14,160,8,64]{1,3,2,0:T(8,128)(2,1)} %copy.84, bf16[14,160,8,64]{1,3,2,0:T(8,128)(2,1)} %copy.80), kind=kOutput, calls=%fused_computation.4 | convolution fusion | flops 381319680 | bytes 27670720 | tf_op jit(solution)/shard_map/cqhd,ckhd->chqk/dot_general | solution.py:448
  270.7 14.5 %multiply_convert_fusion = bf16[14,8,160,160]{2,3,1,0:T(8,128)(2,1)S(1)} fusion(f32[14,8,160,160]{2,3,1,0:T(8,128)} %get-tuple-element.84, f32[14,8,160,160]{2,3,1,0:T(8,128)} %get-tuple-element.76, f32[14,8,160]{2,1,0:T(8,128)S(1)} %get-tuple-element.83, f32[14,8,160]{2,1,0:T(8,128)S(1)} %copy-done.22, pred[14,160]{1,0:T(8,128)(4,1)S(1)} %copy-done.32), kind=kLoop, calls=%fused_computation.3 | loop fusion | flops 17203200 | bytes 28817600 | tf_op jit(solution)/shard_map/convert_element_type | solution.py:449
  292.1 10.0 %fusion.16 = bf16[14,160,8,64]{1,3,2,0:T(8,128)(2,1)} fusion(bf16[14,160,8,64]{1,3,2,0:T(8,128)(2,1)} %copy.78, bf16[14,8,160,160]{2,3,1,0:T(8,128)(2,1)} %copy-done), kind=kOutput, calls=%fused_computation.62 | convolution fusion | flops 369295360 | bytes 10321920 | tf_op jit(solution)/shard_map/chqk,cqhd->ckhd/dot_general | solution.py:453
  302.1 11.0 %convert_reduce_fusion.1 = (f32[8,64]{1,0:T(8,128)S(1)}, bf16[14,8,64,160]{3,2,1,0:T(8,128)(2,1)}) fusion(bf16[14,160,8,64]{1,3,2,0:T(8,128)(2,1)} %copy.84, f32[14,8,160,160]{2,3,1,0:T(8,128)} %get-tuple-element.76, f32[14,8,160]{2,1,0:T(8,128)S(1)} %copy-done.22, pred[14,160]{1,0:T(8,128)(4,1)S(1)} %copy-done.32), kind=kOutput, calls=%fused_computation.25 | convolution fusion | flops 381910528 | bytes 16132288 | tf_op jit(solution)/shard_map/chqk,cqhd->ckhd/dot_general | solution.py:454
  313.1 10.7 %convolution_convert_fusion.3 = bf16[2048,512]{1,0:T(8,128)(2,1)} fusion(bf16[2240,2048]{1,0:T(8,128)(2,1)} %get-tuple-element.35, bf16[2240,512]{1,0:T(8,128)(2,1)S(1)} %get-tuple-element.28), kind=kOutput, calls=%fused_computation.65 | convolution fusion | flops 4698669056 | bytes 13565952 | tf_op jit(solution)/shard_map/dot_general | solution.py:23
  323.9 10.4 %convolution_convert_fusion.2 = bf16[512,2048]{1,0:T(8,128)(2,1)} fusion(bf16[2240,2048]{1,0:T(8,128)(2,1)} %get-tuple-element.90, f32[2240,512]{1,0:T(8,128)S(1)} %bitcast.95, f32[512]{0:T(512)S(1)} %convert_element_type.159, f32[512]{0:T(512)S(1)} %convert_element_type.158, f32[2240]{0:T(1024)S(1)} %fusion.28, f32[2240]{0:T(1024)S(1)} %broadcast_multiply_fusion.1), kind=kOutput, calls=%fused_computation.64 | convolution fusion | flops 4704403456 | bytes 15881728 | tf_op jit(solution)/shard_map/dot_general | solution.py:23
  334.3 4.4 copy.88
  338.7 6.8 %convert_element_type.175 = bf16[2240,512]{0,1:T(8,128)(2,1)S(1)} reshape(bf16[14,160,8,64]{1,0,3,2:T(8,128)(2,1)} %copy.88) | data formatting | bytes 4587520 | tf_op jit(solution)/shard_map/convert_element_type | solution.py:452
  353.5 4.3 copy.91
  357.8 6.6 %convert_element_type.178 = bf16[2240,512]{0,1:T(8,128)(2,1)S(1)} reshape(bf16[14,160,8,64]{1,0,3,2:T(8,128)(2,1)} %copy.91) | data formatting | bytes 4587520 | tf_op jit(solution)/shard_map/convert_element_type | solution.py:453
  364.4 6.3 %copy.94 = bf16[14,160,8,64]{1,0,3,2:T(8,128)(2,1)} copy(bf16[14,160,8,64]{1,3,2,0:T(8,128)(2,1)} %bitcast.98) | data formatting | bytes 4587520 | tf_op jit(solution)/shard_map/convert_element_type | solution.py:454
  370.8 7.8 %convert_element_type.181 = bf16[2240,512]{0,1:T(8,128)(2,1)} reshape(bf16[14,160,8,64]{1,0,3,2:T(8,128)(2,1)} %copy.94) | data formatting | bytes 4587520 | tf_op jit(solution)/shard_map/convert_element_type | solution.py:454
  398.3 6.1 %pad_maximum_fusion.g = bf16[2,3072,512]{2,1,0:T(8,128)(2,1)} fusion(bf16[1,3072,512]{2,1,0:T(8,128)(2,1)} %bitcast.97, bf16[1,3072,512]{2,1,0:T(8,128)(2,1)} %bitcast.96), kind=kLoop, calls=%fused_computation.31 | loop fusion | flops 3145728 | bytes 12582912 | tf_op jit(solution)/shard_map/stack | solution.py:459
  404.5 70.4 %comm.1 = (bf16[3072,512]{1,0:T(8,128)(2,1)S(1)}, f32[16,512]{1,0:T(8,128)S(1)}) custom-call(bf16[2,3072,512]{2,1,0:T(8,128)(2,1)} %pad_maximum_fusion.g, f32[16,512]{1,0:T(8,128)S(1)} %stack.42.small), custom_call_target="tpu_custom_call" | custom-call | tf_op jit(solution)/shard_map/comm/pallas_call | solution.py:380
  480.4 4.7 fusion.9
  (199 shorter events, 105.6 us)
Async XLA Ops:
  7.2 117.5 %all-gather.5.cloned.1.call-start = ((), (), s32[]{:S(2)}) async-start(), calls=%async_computation | async-start | bytes 3145728 | tf_op jit(solution)/shard_map/all_gather | solution.py:405
  7.9 165.0 %all-gather.7.cloned.1.call-start = ((), (), s32[]{:S(2)}) async-start(), calls=%async_computation.1 | async-start | bytes 3145728 | tf_op jit(solution)/shard_map/all_gather | solution.py:405
  24.9 7.3 %copy-start.46 = (s32[28]{0:T(128)S(1)}, s32[28]{0:T(128)}, u32[]{:S(2)}) copy-start(s32[28]{0:T(128)} %param.24) | copy-start | bytes 340
  24.9 7.4 %copy-start.47 = (s32[28]{0:T(128)S(1)}, s32[28]{0:T(128)}, u32[]{:S(2)}) copy-start(s32[28]{0:T(128)} %param.23) | copy-start | bytes 340
  24.9 7.5 %copy-start.48 = (s32[28]{0:T(128)S(1)}, s32[28]{0:T(128)}, u32[]{:S(2)}) copy-start(s32[28]{0:T(128)} %param.22) | copy-start | bytes 340
  24.9 7.6 %copy-start.26 = (bf16[512,256]{1,0:T(8,128)(2,1)S(1)}, bf16[512,256]{1,0:T(8,128)(2,1)}, u32[]{:S(2)}) copy-start(bf16[512,256]{1,0:T(8,128)(2,1)} %param.25) | copy-start | bytes 786436
  24.9 10.0 %copy-start.49 = (bf16[256]{0:T(256)(128)(2,1)S(1)}, bf16[256]{0:T(256)(128)(2,1)}, u32[]{:S(2)}) copy-start(bf16[256]{0:T(256)(128)(2,1)} %param.26) | copy-start | bytes 1540
  43.9 7.3 %copy-start.27 = (bf16[512,256]{1,0:T(8,128)(2,1)S(1)}, bf16[512,256]{1,0:T(8,128)(2,1)}, u32[]{:S(2)}) copy-start(bf16[512,256]{1,0:T(8,128)(2,1)} %param.27) | copy-start | bytes 786436
  68.9 24.6 %copy-start.31 = (pred[14,160]{1,0:T(8,128)(4,1)}, pred[14,160]{1,0:T(8,128)(4,1)S(1)}, u32[]{:S(2)}) copy-start(pred[14,160]{1,0:T(8,128)(4,1)S(1)} %get-tuple-element.74) | copy-start | bytes 6724
  83.0 10.5 %copy-start.6 = (bf16[14,160,8,64]{1,3,2,0:T(8,128)(2,1)S(1)}, bf16[14,160,8,64]{1,3,2,0:T(8,128)(2,1)}, u32[]{:S(2)}) copy-start(bf16[14,160,8,64]{1,3,2,0:T(8,128)(2,1)} %copy.80) | copy-start | bytes 6881284
  93.6 8.6 %copy-start.21 = (f32[14,8,160]{2,1,0:T(8,128)}, f32[14,8,160]{2,1,0:T(8,128)S(1)}, u32[]{:S(2)}) copy-start(f32[14,8,160]{2,1,0:T(8,128)S(1)} %log_add_fusion) | copy-start | bytes 215044
  106.6 7.0 %copy-start.28 = (bf16[256,512]{1,0:T(8,128)(2,1)S(1)}, bf16[256,512]{1,0:T(8,128)(2,1)}, u32[]{:S(2)}) copy-start(bf16[256,512]{1,0:T(8,128)(2,1)} %param.30) | copy-start | bytes 786436
  106.6 9.2 %copy-start.40 = (bf16[512]{0:T(512)(128)(2,1)S(1)}, bf16[512]{0:T(512)(128)(2,1)}, u32[]{:S(2)}) copy-start(bf16[512]{0:T(512)(128)(2,1)} %param.33) | copy-start | bytes 3076
  106.6 9.2 %copy-start.41 = (bf16[512]{0:T(512)(128)(2,1)S(1)}, bf16[512]{0:T(512)(128)(2,1)}, u32[]{:S(2)}) copy-start(bf16[512]{0:T(512)(128)(2,1)} %param.32) | copy-start | bytes 3076
  113.6 5.7 %copy-start.11 = (bf16[2240,512]{0,1:T(8,128)(2,1)}, bf16[2240,512]{0,1:T(8,128)(2,1)S(1)}, u32[]{:S(2)}) copy-start(bf16[2240,512]{0,1:T(8,128)(2,1)S(1)} %convert_element_type.156) | copy-start | bytes 6881284
  119.3 4.3 copy-start.42
  119.3 4.8 copy-start.43
  124.7 48.2 %copy-start.39 = (f32[512]{0:T(512)S(1)}, f32[512]{0:T(512)}, u32[]{:S(2)}) copy-start(f32[512]{0:T(512)} %convert_element_type.163) | copy-start | bytes 6148
  217.9 11.9 %copy-start.30 = (f32[2240]{0:T(1024)S(1)}, f32[2240]{0:T(1024)}, u32[]{:S(2)}) copy-start(f32[2240]{0:T(1024)} %copy-done.29) | copy-start | bytes 26884
  247.9 7.5 %copy-start.22 = (f32[14,8,160]{2,1,0:T(8,128)S(1)}, f32[14,8,160]{2,1,0:T(8,128)}, u32[]{:S(2)}) copy-start(f32[14,8,160]{2,1,0:T(8,128)} %copy-done.21) | copy-start | bytes 215044
  247.9 7.5 %copy-start.32 = (pred[14,160]{1,0:T(8,128)(4,1)S(1)}, pred[14,160]{1,0:T(8,128)(4,1)}, u32[]{:S(2)}) copy-start(pred[14,160]{1,0:T(8,128)(4,1)} %copy-done.31) | copy-start | bytes 6724
  270.7 18.1 %copy-start.1 = (bf16[14,160,8,64]{1,3,2,0:T(8,128)(2,1)S(1)}, bf16[14,160,8,64]{1,3,2,0:T(8,128)(2,1)}, u32[]{:S(2)}) copy-start(bf16[14,160,8,64]{1,3,2,0:T(8,128)(2,1)} %copy.79) | copy-start | bytes 6881284
  302.1 21.8 %slice-start.4 = ((s8[4587520]{0:T(1024)(128)(4,1)}), s8[393216]{0:T(1024)(128)(4,1)S(1)}, s32[]{:S(2)}) async-start(s8[4587520]{0:T(1024)(128)(4,1)} %bitcast.94), calls=%async_computation.6 | async-start | bytes 786432
  313.1 10.7 %slice-start.5 = ((s8[4587520]{0:T(1024)(128)(4,1)}), s8[4194304]{0:T(1024)(128)(4,1)S(1)}, s32[]{:S(2)}) async-start(s8[4587520]{0:T(1024)(128)(4,1)} %bitcast.94), calls=%async_computation.7 | async-start | bytes 8388608
  323.9 10.5 %copy-start.3 = (bf16[14,8,64,160]{3,2,1,0:T(8,128)(2,1)S(1)}, bf16[14,8,64,160]{3,2,1,0:T(8,128)(2,1)}, u32[]{:S(2)}) copy-start(bf16[14,8,64,160]{3,2,1,0:T(8,128)(2,1)} %get-tuple-element.86) | copy-start | bytes 6881284
  338.7 6.8 %copy-start.20 = (bf16[512,512]{1,0:T(8,128)(2,1)S(1)}, bf16[512,512]{1,0:T(8,128)(2,1)}, u32[]{:S(2)}) copy-start(bf16[512,512]{1,0:T(8,128)(2,1)} %copy-done.19) | copy-start | bytes 1572868
  381.6 4.9 copy-start.8
  381.6 4.9 copy-start.45
  398.3 6.1 %copy-start.35 = (f32[512]{0:T(512)S(1)}, f32[512]{0:T(512)}, u32[]{:S(2)}) copy-start(f32[512]{0:T(512)} %get-tuple-element.23) | copy-start | bytes 6148
  398.3 6.1 %copy-start.36 = (f32[512]{0:T(512)S(1)}, f32[512]{0:T(512)}, u32[]{:S(2)}) copy-start(f32[512]{0:T(512)} %get-tuple-element.26) | copy-start | bytes 6148
  398.3 6.1 %copy-start.37 = (f32[512]{0:T(512)S(1)}, f32[512]{0:T(512)}, u32[]{:S(2)}) copy-start(f32[512]{0:T(512)} %get-tuple-element.27) | copy-start | bytes 6148
  404.5 73.9 %slice-start.2 = ((s8[4587520]{0:T(1024)(128)(4,1)}), s8[4194304]{0:T(1024)(128)(4,1)S(1)}, s32[]{:S(2)}) async-start(s8[4587520]{0:T(1024)(128)(4,1)} %bitcast.91), calls=%async_computation.4 | async-start | bytes 8388608
  (26 other events, 63.3 us)
Sparse Core Ops, SparseCore 0:
  9.6 13.2 all-gather.4
  24.4 11.8 all-gather.6

commit v2 on v1

--- a/solution.py
+++ b/solution.py
@@ -12,6 +12,9 @@
 HEAD_DIM = 64
 SEQ = 160
 ROWS = 3072
+SCALE = HEAD_DIM ** (-0.5)
+ATT_BLOCK = 32
+FFN_BLOCK = 256
 EPSILON = 1e-12
 
 
@@ -249,8 +252,8 @@
     def __init__(self, K, g, small, out, sout, bufs, stride=1):
         self.stride = stride
         self.K = K; self.CH = ROWS // K; self.SB = self.CH // 3
-        self.g, self.small, self.out, self.sout = g, small, out, sout
-        (self.core_buf, self.acc, self.r1, self.r2, self.r3, self.r4, self.sm, self.csem, self.rsem, self.asem, self.smsem) = bufs
+        self.g, self.small, self.out_hbm, self.sout = g, small, out, sout
+        (self.core_buf, self.acc, self.r1, self.r2, self.r3, self.r4, self.out, self.sm, self.csem, self.rsem, self.asem, self.smsem, self.fsem) = bufs
         dp = lax.axis_index("dp"); t = lax.axis_index("tensor")
         self.t = t
         x = lax.rem(dp, 2); y = lax.rem(dp // 2, 2); p = lax.rem(dp // 4, 2); q = dp // 8
@@ -328,6 +331,10 @@
             for r in range(3):
                 self.ag(k, r, i).wait_recv()
                 if i > 0: self.ag(k, r, i - 1).start()
+            if i == 0: self.final_copy(k).start()
+    def final_copy(self, k):
+        sl = pl.ds(k * self.CH, self.CH)
+        return pltpu.make_async_copy(self.out.at[sl], self.out_hbm.at[sl], self.fsem.at[k])
     def small_stage(self, i):
         if i > 0:
             self.small_copy(i - 1).wait_recv()
@@ -349,7 +356,7 @@
     def iterations(self): return self.K + (self.NSTAGE - 1) * self.stride
     def finish(self):
         def body(k, c):
-            self.core_copy(k).wait_send()
+            self.core_copy(k).wait_send(); self.final_copy(k).wait()
             for r in range(3):
                 for i in range(4):
                     self.rs(k, r, i).wait_send(); self.ag(k, r, i).wait_send()
@@ -363,29 +370,469 @@
         return [pltpu.VMEM((K, 3 * SB, 512), bf16), pltpu.VMEM((ROWS, 512), bf16),
             pltpu.VMEM((K, 3, SB // 2, 512), bf16), pltpu.VMEM((K, 3, SB // 4, 512), bf16),
             pltpu.VMEM((K, 3, SB // 4, 256), bf16), pltpu.VMEM((K, 3, SB // 4, 128), bf16),
-            pltpu.VMEM((2, 5, S, 512), f32),
-            D((2, K)), D((2, 4, K, 3)), D((2, 4, K, 3)), D((2, 5))]
-
-def kern(K, stride, g, small, out, sout, *bufs):
-    c = Comm(K, g, small, out, sout, bufs, stride)
-    c.barrier()
-    def body(it, _):
-        c.iteration(it); return _
-    lax.fori_loop(0, c.iterations, body, 0)
-    c.finish()
-
-def comm(g, small, K=8, stride=1):
-    S = small.shape[0]
-    V = pl.BlockSpec(memory_space=pltpu.VMEM)
-    return pl.pallas_call(functools.partial(kern, K, stride),
-        out_shape=(jax.ShapeDtypeStruct((ROWS, 512), bf16), jax.ShapeDtypeStruct((S, 512), f32)),
-        in_specs=[V, V], out_specs=(V, V), scratch_shapes=Comm.scratch(K, S),
-        compiler_params=pltpu.CompilerParams(collective_id=0, has_side_effects=True, vmem_limit_bytes=50 << 20), name="comm")(g, small)
-
-
-def pack_half(dq, dk, dv, do, di, dd):
-    vo = jnp.concatenate([dv, jnp.concatenate([do[:, :256], do[:, 256:]], axis=0)], axis=1)
-    return jnp.concatenate([dd, di[:, :512], di[:, 512:], jnp.concatenate([dq, dk], axis=1), vo], axis=0)
+            pltpu.VMEM((ROWS, 512), bf16), pltpu.VMEM((2, 5, S, 512), f32),
+            D((2, K)), D((2, 4, K, 3)), D((2, 4, K, 3)), D((2, 5)), D((K,))]
+
+
+def gather_kernel(
+    x_ref, wq_ref, wk_ref, wv_ref, bq_ref, bv_ref, bi_ref, wo_ref, wi_ref, wd_ref,
+    q_ref, k_ref, v_ref, wqkv_out, wo_out, wi_out, wd_out, bias_out,
+    wqkv, bias, near, sent, came,
+):
+    step = pl.program_id(0)
+    dp, t = lax.axis_index("dp"), lax.axis_index("tensor")
+
+    def pair(i, src, dst):
+        return pltpu.make_async_remote_copy(
+            src_ref=src, dst_ref=dst, send_sem=sent.at[i], recv_sem=came.at[i],
+            device_id=(dp, 1 - t), device_id_type=MESH,
+        )
+
+    first = [
+        pair(0, wq_ref, wqkv.at[t, 0]), pair(1, wk_ref, wqkv.at[t, 1]), pair(2, wv_ref, wqkv.at[t, 2]),
+        pair(3, bias.at[t], bias.at[t]),
+    ]
+    later = [pair(4, wo_ref, wo_out.at[t]), pair(5, wi_ref, wi_out.at[t]), pair(6, wd_ref, wd_out.at[t])]
+    own = [
+        pltpu.make_async_copy(wo_ref, wo_out.at[t], near.at[0]),
+        pltpu.make_async_copy(wi_ref, wi_out.at[t], near.at[1]),
+        pltpu.make_async_copy(wd_ref, wd_out.at[t], near.at[2]),
+    ]
+    keep = [pltpu.make_async_copy(wqkv, wqkv_out, near.at[3]), pltpu.make_async_copy(bias, bias_out, near.at[4])]
+
+    @pl.when(step == 0)
+    def _():
+        barrier = pltpu.get_barrier_semaphore()
+        pl.semaphore_signal(barrier, inc=1, device_id=(dp, 1 - t), device_id_type=MESH)
+        bias[t, 0:1] = bq_ref[...].astype(f32)
+        bias[t, 1:2] = bv_ref[...].astype(f32)
+        for i in range(4):
+            bias[t, 2 + i : 3 + i] = bi_ref[:, 256 * i : 256 * i + 256].astype(f32)
+        bias[t, 6:8] = jnp.zeros((2, 256), f32)
+        pl.semaphore_wait(barrier, 1)
+        for copy in first + later:
+            copy.start()
+        for copy in own:
+            copy.start()
+        for j, ref in enumerate((wq_ref, wk_ref, wv_ref)):
+            wqkv[t, j] = ref[...]
+        for copy in first:
+            copy.wait_recv()
+        for copy in keep:
+            copy.start()
+
+    x = x_ref[...]
+    for h in range(2):
+        cols = slice(256 * h, 256 * h + 256)
+        q_ref[:, cols] = ((product(x, wqkv[h, 0]) + bias[h, 0:1]).astype(bf16).astype(f32) * SCALE).astype(bf16)
+        k_ref[:, cols] = product(x, wqkv[h, 1]).astype(bf16)
+        v_ref[:, cols] = (product(x, wqkv[h, 2]) + bias[h, 1:2]).astype(bf16)
+
+    @pl.when(step == pl.num_programs(0) - 1)
+    def _():
+        for copy in first:
+            copy.wait_send()
+        for copy in later:
+            copy.wait()
+        for copy in own + keep:
+            copy.wait()
+
+
+def gather(states, wq, wk, wv, bq, bv, bi, wo, wi, wd):
+    rows = states.shape[0]
+    block = 2 * SEQ
+    whole = lambda a: pl.BlockSpec(a.shape, lambda i: (0,) * a.ndim)
+    tile = pl.BlockSpec((block, 512), lambda i: (i, 0))
+    hbm = pl.BlockSpec(memory_space=pl.ANY)
+    D = pltpu.SemaphoreType.DMA
+    S = jax.ShapeDtypeStruct
+    return pl.pallas_call(
+        gather_kernel,
+        grid=(rows // block,),
+        in_specs=[tile, whole(wq), whole(wk), whole(wv), whole(bq), whole(bv), whole(bi), hbm, hbm, hbm],
+        out_specs=[tile, tile, tile, hbm, hbm, hbm, hbm, hbm],
+        out_shape=[S((rows, 512), bf16)] * 3 + [
+            S((2, 3, 512, 256), bf16), S((2, 256, 512), bf16), S((2, 512, 1024), bf16), S((2, 1024, 512), bf16), S((2, 8, 256), f32),
+        ],
+        scratch_shapes=[pltpu.VMEM((2, 3, 512, 256), bf16), pltpu.VMEM((2, 8, 256), f32), D((5,)), D((7,)), D((7,))],
+        compiler_params=pltpu.CompilerParams(collective_id=1, has_side_effects=True, vmem_limit_bytes=60 << 20),
+        name="gather",
+    )(states, wq, wk, wv, bq, bv, bi, wo, wi, wd)
+
+
+def select_heads(full, block, heads):
+    out = full[3 * block :]
+    for h in (2, 1, 0):
+        out = jnp.where(heads[:block] == h, full[h * block : (h + 1) * block], out)
+    return out
+
+
+def spread_heads(rows, block, own):
+    return jnp.where(own, jnp.concatenate([rows] * 4, axis=0), jnp.zeros((), rows.dtype))
+
+
+def normal_parts(h):
+    a = jnp.abs(h)
+    u = 1.0 / (1.0 + (0.3275911 * 0.7071067811865476) * a)
+    bell = jnp.exp(-0.5 * h * h)
+    poly = u * (0.254829592 + u * (-0.284496736 + u * (1.421413741 + u * (-1.453152027 + u * 1.061405429))))
+    tail = 0.5 * poly * bell
+    return jnp.where(h < 0, tail, 1.0 - tail), bell * 0.3989422804014327
+
+
+def row_mean(a):
+    return jnp.sum(a, axis=-1, keepdims=True) * (1.0 / 512)
+
+
+def chain_scalars(len_ref, start_ref, end_ref, c):
+    length = len_ref[c]
+    start = start_ref[c]
+    end = jnp.minimum(end_ref[c], length)
+    return length, start, end
+
+
+def live_kernel(
+    len_ref, start_ref, end_ref,
+    x_ref, cot_ref, q_ref, k_ref, v_ref, wo_hbm, wi_hbm, wd_hbm, bias_ref, vec_ref,
+    g_out, small_out, dq_ref, dk_ref, dv_ref, gf_ref,
+    wo, wi, wd, context, inputs, upstream, first, x_all, dk_all, dv_all, acc_k, acc_v, acc_d, acc_i, acc_o, acc_s, gelu_grad, act, stage, off, sems,
+):
+    step = pl.program_id(0)
+    chains = len_ref.shape[0] // 2
+    t = lax.axis_index("tensor")
+    B = ATT_BLOCK
+    R = FFN_BLOCK
+    PAD = 32
+    loads = [pltpu.make_async_copy(a, b, sems.at[i]) for i, (a, b) in enumerate(((wo_hbm, wo), (wi_hbm, wi), (wd_hbm, wd)))]
+    heads = lax.broadcasted_iota(jnp.int32, (4 * B, 256), 1) // HEAD_DIM
+    own = heads == lax.broadcasted_iota(jnp.int32, (4 * B, 256), 0) // B
+
+    @pl.when(step == 0)
+    def _():
+        for copy in loads:
+            copy.start()
+        off[0] = 0
+        acc_d[...] = jnp.zeros_like(acc_d)
+        acc_i[...] = jnp.zeros_like(acc_i)
+        acc_o[...] = jnp.zeros_like(acc_o)
+        acc_s[...] = jnp.zeros_like(acc_s)
+
+    def blocks_of(c):
+        length, start, end = chain_scalars(len_ref, start_ref, end_ref, t * chains + c)
+        r16 = (start // 16) * 16
+        b0 = start // B
+        b1 = jnp.where(end > start, (end + B - 1) // B, b0)
+        return length, start, end, r16, b0, b1
+
+    def probabilities(q, k, length):
+        qs = spread_heads(q, B, own)
+        scores = product_right(qs, k)
+        scores = jnp.where(lax.broadcasted_iota(jnp.int32, scores.shape, 1) < length, scores, -1e9)
+        e = jnp.exp(scores - jnp.max(scores, axis=-1, keepdims=True))
+        return qs, e * (1.0 / jnp.sum(e, axis=-1, keepdims=True))
+
+    @pl.when(step < chains)
+    def _forward():
+        c = step
+        length, start, end, r16, b0, b1 = blocks_of(c)
+        base = off[c] + PAD - r16
+        off[c + 1] = off[c] + jnp.where(end > start, ((end + 15) // 16) * 16 - r16, 0)
+        x_all[pl.ds(c * SEQ, SEQ)] = x_ref[...]
+
+        def block(b, carry):
+            p0 = pl.multiple_of(b * B, B)
+            out = []
+            for g in range(2):
+                cols = slice(256 * g, 256 * g + 256)
+                _, p = probabilities(q_ref[pl.ds(p0, B), cols], k_ref[:, cols], length)
+                out.append(select_heads(product(p.astype(bf16), v_ref[:, cols]), B, heads))
+            ctx = jnp.concatenate(out, axis=1).astype(bf16)
+            pos = p0 + lax.broadcasted_iota(jnp.int32, (B, 512), 0)
+            live = (pos >= start) & (pos < end)
+            cot = jnp.where(live, cot_ref[pl.ds(p0, B)].astype(f32), 0.0).astype(bf16)
+            x = x_ref[pl.ds(p0, B)]
+            for i in range(B // 16):
+                @pl.when(p0 + 16 * i >= r16)
+                def _(i=i):
+                    dst = pl.ds(pl.multiple_of(base + p0 + 16 * i, 16), 16)
+                    rows = slice(16 * i, 16 * i + 16)
+                    context[dst] = ctx[rows]
+                    inputs[dst] = x[rows]
+                    upstream[dst] = cot[rows]
+            return carry
+
+        lax.fori_loop(b0, b1, block, 0)
+
+    @pl.when(step == chains)
+    def _feed_forward():
+        n = off[chains]
+        tail = pl.ds(pl.multiple_of(PAD + n, 16), R)
+        for ref in (context, inputs, upstream):
+            ref[tail] = jnp.zeros((R, 512), bf16)
+        for copy in loads:
+            copy.wait()
+        vec = vec_ref[...].astype(f32)
+        bo, g1, s1, bd, g2, s2 = (vec[i : i + 1] for i in range(6))
+
+        def block(b, carry):
+            rows = pl.ds(pl.multiple_of(PAD + b * R, 16), R)
+            ctx = context[rows]
+            attended = product(ctx[:, :256], wo[0]) + product(ctx[:, 256:], wo[1]) + bo
+            s = inputs[rows].astype(f32) + attended
+            center = s - row_mean(s)
+            rstd1 = lax.rsqrt(row_mean(center * center) + EPSILON)
+            hat1 = center * rstd1
+            normed = hat1 * g1 + s1
+            low = normed.astype(bf16)
+            branch = jnp.zeros((R, 512), f32) + bd
+            for j in range(4):
+                h, o = j // 2, 512 * (j % 2)
+                bi = jnp.concatenate([bias_ref[h, 2 + o // 256 : 3 + o // 256], bias_ref[h, 3 + o // 256 : 4 + o // 256]], axis=1)
+                hid = product(low, wi[h, :, o : o + 512]) + bi
+                cdf, pdf = normal_parts(hid)
+                a = (hid * cdf).astype(bf16)
+                gelu_grad[j] = cdf + hid * pdf
+                act[j] = a
+                branch = branch + product(a, wd[h, o : o + 512])
+            s = normed + branch
+            center = s - row_mean(s)
+            rstd2 = lax.rsqrt(row_mean(center * center) + EPSILON)
+            hat2 = center * rstd2
+            up = upstream[rows].astype(f32)
+            gy = up * g2
+            grad = rstd2 * (gy - row_mean(gy) - hat2 * row_mean(gy * hat2))
+            gb = grad.astype(bf16)
+            gn = grad
+            for j in range(4):
+                h, o = j // 2, 512 * (j % 2)
+                gh = (product_right(gb, wd[h, o : o + 512]) * gelu_grad[j]).astype(bf16)
+                acc_d[h, o : o + 512] += product_left(act[j], gb)
+                acc_i[j] += product_left(low, gh)
+                acc_s[8 + j : 9 + j] += jnp.sum(gh.astype(f32), axis=0, keepdims=True)
+                gn = gn + product_right(gh, wi[h, :, o : o + 512])
+            acc_s[1:2] += jnp.sum(gn * hat1, axis=0, keepdims=True)
+            acc_s[2:3] += jnp.sum(gn, axis=0, keepdims=True)
+            acc_s[3:4] += jnp.sum(gb.astype(f32), axis=0, keepdims=True)
+            acc_s[4:5] += jnp.sum(up * hat2, axis=0, keepdims=True)
+            acc_s[5:6] += jnp.sum(up, axis=0, keepdims=True)
+            gy = gn * g1
+            grad = rstd1 * (gy - row_mean(gy) - hat1 * row_mean(gy * hat1))
+            first[rows] = grad
+            ga = grad.astype(bf16)
+            acc_s[0:1] += jnp.sum(ga.astype(f32), axis=0, keepdims=True)
+            acc_o[...] += product_left(ctx, ga)
+            upstream[rows] = jnp.concatenate([product_right(ga, wo[0]), product_right(ga, wo[1])], axis=1).astype(bf16)
+            return carry
+
+        lax.fori_loop(0, (n + R - 1) // R, block, 0)
+        for h in range(2):
+            stage[h, 0:1024] = acc_d[h].astype(bf16)
+            stage[h, 1024:1536] = acc_i[2 * h].astype(bf16)
+            stage[h, 1536:2048] = acc_i[2 * h + 1].astype(bf16)
+            pltpu.make_async_copy(stage.at[h, pl.ds(0, 2048)], g_out.at[h, pl.ds(0, 2048)], sems.at[3 + h]).start()
+            stage[h, 2560:2816, 256:512] = acc_o[256 * h : 256 * h + 256, 0:256].astype(bf16)
+            stage[h, 2816:3072, 256:512] = acc_o[256 * h : 256 * h + 256, 256:512].astype(bf16)
+
+    @pl.when(step > chains)
+    def _backward():
+        c = step - chains - 1
+        length, start, end, r16, b0, b1 = blocks_of(c)
+        base = off[c] + PAD - r16
+        acc_k[...] = jnp.zeros_like(acc_k)
+        acc_v[...] = jnp.zeros_like(acc_v)
+        dq_ref[...] = jnp.zeros_like(dq_ref)
+        gf_ref[...] = jnp.zeros_like(gf_ref)
+
+        def block(b, carry):
+            p0 = pl.multiple_of(b * B, B)
+            src = pl.ds(pl.multiple_of(base + p0, 16), B)
+            pos = p0 + lax.broadcasted_iota(jnp.int32, (B, 512), 0)
+            live = (pos >= start) & (pos < end)
+            gc = jnp.where(live, upstream[src].astype(f32), 0.0).astype(bf16)
+            out = []
+            for g in range(2):
+                cols = slice(256 * g, 256 * g + 256)
+                qs, p = probabilities(q_ref[pl.ds(p0, B), cols], k_ref[:, cols], length)
+                gs = spread_heads(gc[:, cols], B, own)
+                gp = product_right(gs, v_ref[:, cols])
+                ds = (p * (gp - jnp.sum(p * gp, axis=-1, keepdims=True))).astype(bf16)
+                out.append(select_heads(product(ds, k_ref[:, cols]), B, heads) * SCALE)
+                acc_k[:, cols] += product_left(ds, qs)
+                acc_v[:, cols] += product_left(p.astype(bf16), gs)
+            dq = jnp.concatenate(out, axis=1).astype(bf16)
+            dq_ref[pl.ds(p0, B)] = dq
+            gf_ref[pl.ds(p0, B)] = jnp.where(live, first[src], 0.0)
+            for i in range(B // 16):
+                @pl.when(p0 + 16 * i >= r16)
+                def _(i=i):
+                    dst = pl.ds(pl.multiple_of(base + p0 + 16 * i, 16), 16)
+                    context[dst] = dq[16 * i : 16 * i + 16]
+            return carry
+
+        lax.fori_loop(b0, b1, block, 0)
+        dk_ref[...] = acc_k[...].astype(bf16)
+        dv_ref[...] = acc_v[...].astype(bf16)
+        rows = pl.ds(c * SEQ, SEQ)
+        dk_all[rows] = dk_ref[...]
+        dv_all[rows] = dv_ref[...]
+
+    @pl.when(step == 2 * chains)
+    def _weights():
+        n = off[chains]
+        context[pl.ds(pl.multiple_of(PAD + n, 16), R)] = jnp.zeros((R, 512), bf16)
+        acc_o[...] = jnp.zeros_like(acc_o)
+
+        def block(b, carry):
+            rows = pl.ds(pl.multiple_of(PAD + b * R, 16), R)
+            dq = context[rows]
+            acc_o[...] += product_left(inputs[rows], dq)
+            acc_s[6:7] += jnp.sum(dq.astype(f32), axis=0, keepdims=True)
+            return carry
+
+        lax.fori_loop(0, (n + R - 1) // R, block, 0)
+        acc_s[7:8] = jnp.sum(dv_all[...].astype(f32), axis=0, keepdims=True)
+        dk = product_left(x_all[...], dk_all[...])
+        dv = product_left(x_all[...], dv_all[...])
+        for h in range(2):
+            cols = slice(256 * h, 256 * h + 256)
+            stage[h, 2048:2560, 0:256] = acc_o[:, cols].astype(bf16)
+            stage[h, 2048:2560, 256:512] = dk[:, cols].astype(bf16)
+            stage[h, 2560:3072, 0:256] = dv[:, cols].astype(bf16)
+            pltpu.make_async_copy(stage.at[h, pl.ds(2048, 1024)], g_out.at[h, pl.ds(2048, 1024)], sems.at[5 + h]).start()
+        small_out[...] = acc_s[...]
+        for h in range(2):
+            pltpu.make_async_copy(stage.at[h, pl.ds(0, 2048)], g_out.at[h, pl.ds(0, 2048)], sems.at[3 + h]).wait()
+            pltpu.make_async_copy(stage.at[h, pl.ds(2048, 1024)], g_out.at[h, pl.ds(2048, 1024)], sems.at[5 + h]).wait()
+
+
+def live_rows(lengths, starts, ends, states, cotangent, q, k, v, wo, wi, wd, bias, vec):
+    rows = states.shape[0]
+    chains = rows // SEQ
+    R = FFN_BLOCK
+    C = rows + 32 + R
+    twice = lambda i, *_: (jnp.where(i < chains, i, jnp.maximum(i - chains - 1, 0)), 0)
+    ahead = lambda i, *_: (jnp.minimum(i, chains - 1), 0)
+    after = lambda i, *_: (jnp.maximum(i - chains - 1, 0), 0)
+    tile = lambda f: pl.BlockSpec((SEQ, 512), f)
+    whole = lambda a: pl.BlockSpec(a.shape, lambda i, *_: (0,) * a.ndim)
+    hbm = pl.BlockSpec(memory_space=pl.ANY)
+    S, V = jax.ShapeDtypeStruct, pltpu.VMEM
+    return pl.pallas_call(
+        live_kernel,
+        grid_spec=pltpu.PrefetchScalarGridSpec(
+            num_scalar_prefetch=3,
+            grid=(2 * chains + 1,),
+            in_specs=[tile(ahead), tile(ahead), tile(twice), tile(twice), tile(twice), hbm, hbm, hbm, whole(bias), whole(vec)],
+            out_specs=[hbm, pl.BlockSpec((16, 512), lambda i, *_: (0, 0)), tile(after), tile(after), tile(after), tile(after)],
+            scratch_shapes=[
+                V((2, 256, 512), bf16), V((2, 512, 1024), bf16), V((2, 1024, 512), bf16),
+                V((C, 512), bf16), V((C, 512), bf16), V((C, 512), bf16), V((C, 512), f32),
+                V((rows, 512), bf16), V((rows, 512), bf16), V((rows, 512), bf16),
+                V((SEQ, 512), f32), V((SEQ, 512), f32),
+                V((2, 1024, 512), f32), V((4, 512, 512), f32), V((512, 512), f32), V((16, 512), f32),
+                V((4, R, 512), f32), V((4, R, 512), bf16), V((2, 3072, 512), bf16),
+                pltpu.SMEM((chains + 1,), jnp.int32), pltpu.SemaphoreType.DMA((7,)),
+            ],
+        ),
+        out_shape=[S((2, 3072, 512), bf16), S((16, 512), f32)] + [S((rows, 512), bf16)] * 3 + [S((rows, 512), f32)],
+        compiler_params=pltpu.CompilerParams(vmem_limit_bytes=62 << 20),
+        name="live_rows",
+    )(lengths, starts, ends, states, cotangent, q, k, v, wo, wi, wd, bias, vec)
+
+
+def rest_kernel(
+    SLOTS, K, STRIDE,
+    g, small, x_ref, q_ref, k_ref, v_ref, len_ref, dq_ref, dk_ref, dv_ref, gf_ref, wqkv, wo, wi, wd, bias_ref, vec_ref,
+    out, sout, y_ref, dx_ref, *bufs,
+):
+    step = pl.program_id(0)
+    comm = Comm(K, g, small, out, sout, bufs, STRIDE)
+    slots = SLOTS
+    done = 0
+
+    def slot(i):
+        it = step * slots + i
+
+        @pl.when(it < comm.iterations)
+        def _():
+            comm.iteration(it)
+
+    @pl.when(step == 0)
+    def _():
+        comm.barrier()
+
+    vec = vec_ref[...].astype(f32)
+    bo, g1, s1, bd, g2, s2 = (vec[i : i + 1] for i in range(6))
+    heads = lax.broadcasted_iota(jnp.int32, (4 * SEQ, 256), 1) // HEAD_DIM
+    ctx = []
+    for c in range(2):
+        rows = slice(c * SEQ, c * SEQ + SEQ)
+        length = len_ref[rows, 0:1]
+        slot(c)
+        parts = []
+        for g_ in range(8):
+            cols = slice(64 * g_, 64 * g_ + 64)
+            scores = product_right(q_ref[rows, cols], k_ref[rows, cols])
+            scores = jnp.where(lax.broadcasted_iota(jnp.int32, scores.shape, 1) < length, scores, -1e9)
+            e = jnp.exp(scores - jnp.max(scores, axis=-1, keepdims=True))
+            p = e * (1.0 / jnp.sum(e, axis=-1, keepdims=True))
+            parts.append(product(p.astype(bf16), v_ref[rows, cols]))
+        ctx.append(jnp.concatenate(parts, axis=1).astype(bf16))
+    ctx = jnp.concatenate(ctx, axis=0)
+    slot(2)
+    s = x_ref[...].astype(f32) + (product(ctx[:, :256], wo[0]) + product(ctx[:, 256:], wo[1]) + bo)
+    center = s - row_mean(s)
+    normed = center * lax.rsqrt(row_mean(center * center) + EPSILON) * g1 + s1
+    low = normed.astype(bf16)
+    branch = bd
+    for j in range(4):
+        h, o = j // 2, 512 * (j % 2)
+        bi = jnp.concatenate([bias_ref[h, 2 + o // 256 : 3 + o // 256], bias_ref[h, 3 + o // 256 : 4 + o // 256]], axis=1)
+        hid = product(low, wi[h, :, o : o + 512]) + bi
+        cdf, _ = normal_parts(hid)
+        branch = branch + product((hid * cdf).astype(bf16), wd[h, o : o + 512])
+        if j == 1:
+            slot(3)
+    s = normed + branch
+    center = s - row_mean(s)
+    y_ref[...] = (center * lax.rsqrt(row_mean(center * center) + EPSILON) * g2 + s2).astype(bf16)
+    slot(4)
+    dx = gf_ref[...]
+    for h in range(2):
+        cols = slice(256 * h, 256 * h + 256)
+        for j, ref in enumerate((dq_ref, dk_ref, dv_ref)):
+            dx = dx + product_right(ref[:, cols], wqkv[h, j])
+    dx_ref[...] = dx
+
+    @pl.when(step == pl.num_programs(0) - 1)
+    def _():
+        def body(it, carry):
+            comm.iteration(it)
+            return carry
+
+        lax.fori_loop(slots * pl.num_programs(0), comm.iterations, body, 0)
+        comm.finish()
+
+
+def rest(g, small, states, q, k, v, lens, dq, dk, dv, gf, wqkv, wo, wi, wd, bias, vec):
+    rows = states.shape[0]
+    block = 2 * SEQ
+    K, STRIDE, SLOTS = 8, 2, 5
+    tile = pl.BlockSpec((block, 512), lambda i: (i, 0))
+    whole = lambda a: pl.BlockSpec(a.shape, lambda i: (0,) * a.ndim)
+    vm = pl.BlockSpec(memory_space=pltpu.VMEM)
+    S = jax.ShapeDtypeStruct
+    return pl.pallas_call(
+        functools.partial(rest_kernel, SLOTS, K, STRIDE),
+        grid=(rows // block,),
+        in_specs=[vm, vm, tile, tile, tile, tile, pl.BlockSpec((block, 128), lambda i: (i, 0)), tile, tile, tile, tile,
+                  whole(wqkv), whole(wo), whole(wi), whole(wd), whole(bias), whole(vec)],
+        out_specs=[pl.BlockSpec(memory_space=pl.ANY), vm, tile, tile],
+        out_shape=[S((ROWS, 512), bf16), S(small.shape, f32), S((rows, 512), bf16), S((rows, 512), f32)],
+        scratch_shapes=Comm.scratch(K, small.shape[0]),
+        compiler_params=pltpu.CompilerParams(collective_id=0, has_side_effects=True, vmem_limit_bytes=61 << 20),
+        name="rest",
+    )(g, small, states, q, k, v, lens, dq, dk, dv, gf, wqkv, wo, wi, wd, bias, vec)
 
 
 def unpack_half(w):
@@ -402,73 +849,22 @@
     output_weight, output_bias, first_gain, first_shift, inner_weight, inner_bias, down_weight, down_bias, second_gain, second_shift,
 ):
     t = lax.axis_index("tensor")
-    gather = lambda a, axis: lax.all_gather(a, "tensor", axis=axis, tiled=True)
-    wq, wk, wv = gather(query_weight, 1), gather(key_weight, 1), gather(value_weight, 1)
-    wo, wi, wd = gather(output_weight, 0), gather(inner_weight, 1), gather(down_weight, 0)
-    bq, bv, bi = gather(query_bias, 0), gather(value_bias, 0), gather(inner_bias, 0)
     rows = states.shape[0]
     chains = rows // SEQ
-    heads = wq.shape[1] // HEAD_DIM
-    mine = lambda a: lax.dynamic_slice_in_dim(a, t * chains, chains)
-    lengths, span_starts, span_ends = mine(lengths), mine(span_starts), mine(span_ends)
-    layout = (chains, SEQ, heads, HEAD_DIM)
-    queries = (product(states, wq) + bq).astype(bf16).reshape(layout)
-    keys = product(states, wk).astype(bf16).reshape(layout)
-    values = (product(states, wv) + bv).astype(bf16).reshape(layout)
-    key_live = jnp.arange(SEQ, dtype=jnp.int32)[None, :] < lengths[:, None]
-    scores = attention_scores(queries, keys, key_live)
-    highest = jnp.max(scores, axis=-1, keepdims=True)
-    logsum = highest + jnp.log(jnp.sum(jnp.exp(scores - highest), axis=-1, keepdims=True))
-    probs = jnp.exp(scores - logsum)
-    probs_low = probs.astype(bf16)
-    context = jnp.einsum("chqk,ckhd->cqhd", probs_low, values, preferred_element_type=f32)
-    context = context.reshape(rows, heads * HEAD_DIM).astype(bf16)
-    first_sum = states.astype(f32) + product(context, wo) + output_bias.astype(f32)
-    normed, first_pull = jax.vjp(layer_norm, first_sum, first_gain.astype(f32), first_shift.astype(f32))
-    normed_low = normed.astype(bf16)
-    hidden = product(normed_low, wi) + bi.astype(f32)
-    activation, gelu_pull = jax.vjp(exact_gelu, hidden)
-    activation_low = activation.astype(bf16)
-    second_sum = normed + product(activation_low, wd) + down_bias.astype(f32)
-    output, second_pull = jax.vjp(layer_norm, second_sum, second_gain.astype(f32), second_shift.astype(f32))
-    position = jnp.arange(SEQ, dtype=jnp.int32)[None, :]
-    live = (position >= span_starts[:, None]) & (position < span_ends[:, None]) & key_live
-    grad_out = jnp.where(live.reshape(rows, 1), cotangent.astype(f32), 0.0)
-    grad_second, second_gain_part, second_shift_part = second_pull(grad_out)
-    grad_branch = grad_second.astype(bf16)
-    down_weight_part = product_left(activation_low, grad_branch)
-    (grad_hidden,) = gelu_pull(product_right(grad_branch, wd))
-    grad_hidden = grad_hidden.astype(bf16)
-    inner_weight_part = product_left(normed_low, grad_hidden)
-    grad_normed = product_right(grad_hidden, wi) + grad_second
-    grad_first, first_gain_part, first_shift_part = first_pull(grad_normed)
-    grad_attended = grad_first.astype(bf16)
-    output_weight_part = product_left(context, grad_attended)
-    grad_context = product_right(grad_attended, wo).astype(bf16).reshape(layout)
-    grad_probs = jnp.einsum("cqhd,ckhd->chqk", grad_context, values, preferred_element_type=f32)
-    grad_scores = (probs * (grad_probs - jnp.sum(probs * grad_probs, axis=-1, keepdims=True))).astype(bf16)
-    scale = HEAD_DIM ** (-0.5)
-    flat = (rows, heads * HEAD_DIM)
-    grad_queries = (jnp.einsum("chqk,ckhd->cqhd", grad_scores, keys, preferred_element_type=f32) * scale).reshape(flat).astype(bf16)
-    grad_keys = (jnp.einsum("chqk,cqhd->ckhd", grad_scores, queries, preferred_element_type=f32) * scale).reshape(flat).astype(bf16)
-    grad_values = jnp.einsum("chqk,cqhd->ckhd", probs_low, grad_context, preferred_element_type=f32).reshape(flat).astype(bf16)
-    query_weight_part = product_left(states, grad_queries)
-    key_weight_part = product_left(states, grad_keys)
-    value_weight_part = product_left(states, grad_values)
-    input_grad = product_right(grad_queries, wq) + product_right(grad_keys, wk) + product_right(grad_values, wv) + grad_first
-    halves = jnp.stack([
-        pack_half(query_weight_part[:, a * 256:a * 256 + 256], key_weight_part[:, a * 256:a * 256 + 256],
-                  value_weight_part[:, a * 256:a * 256 + 256], output_weight_part[a * 256:a * 256 + 256],
-                  inner_weight_part[:, a * 1024:a * 1024 + 1024], down_weight_part[a * 1024:a * 1024 + 1024])
-        for a in (0, 1)]).astype(bf16)
-    small = jnp.stack([
-        column_sum(grad_attended), first_gain_part, first_shift_part, column_sum(grad_branch), second_gain_part, second_shift_part,
-        column_sum(grad_queries), column_sum(grad_values), *column_sum(grad_hidden).reshape(4, 512)] + [jnp.zeros((512,), f32)] * 4)
-    summed, small = comm(halves, small, 4, 2)
-    w = {k: v.astype(f32) for k, v in unpack_half(summed).items()}
-    half = lambda row: lax.dynamic_slice_in_dim(row, t * 256, 256)
+    row = lambda a: a.reshape(1, -1)
+    q, k, v, wqkv, wo, wi, wd, bias = gather(
+        states, query_weight, key_weight, value_weight, row(query_bias), row(value_bias), row(inner_bias),
+        output_weight, inner_weight, down_weight,
+    )
+    vec = jnp.stack([output_bias, first_gain, first_shift, down_bias, second_gain, second_shift] + [jnp.zeros((512,), bf16)] * 2)
+    g, small, dq, dk, dv, gf = live_rows(lengths, span_starts, span_ends, states, cotangent, q, k, v, wo, wi, wd, bias, vec)
+    mine = lax.dynamic_slice_in_dim(lengths, t * chains, chains)
+    lens = jnp.broadcast_to(jnp.repeat(mine, SEQ)[:, None], (rows, 128))
+    summed, small, output, input_grad = rest(g, small, states, q, k, v, lens, dq, dk, dv, gf, wqkv, wo, wi, wd, bias, vec)
+    w = {name: part.astype(f32) for name, part in unpack_half(summed).items()}
+    half = lambda line: lax.dynamic_slice_in_dim(line, t * 256, 256)
     return (
-        output.astype(bf16), input_grad, w["query"], half(small[6]), w["key"], w["value"], half(small[7]), w["output"],
+        output, input_grad, w["query"], half(small[6]), w["key"], w["value"], half(small[7]), w["output"],
         small[0], small[1], small[2], w["inner"], lax.dynamic_slice_in_dim(small[8:12].reshape(2048), t * 1024, 1024),
         w["down"], small[3], small[4], small[5],
     )

time: 503 us -> 289 us (0.57); the launches traced: 496 us -> 294 us
  matrix products: 210 us -> 0 us
  Pallas kernels: 70.4 us -> 270 us
  local copies, waits for them, and re-layouts: 125 us -> 17.3 us
  other arithmetic: 60.6 us -> 5.22 us
  blocking collectives: 14.8 us -> 0 us
  between operations: 14.9 us -> 0.84 us
    dot_general x24 -> x0, matrix products: 210 us -> none  [the longest x6 72.6 us: product(): return jnp.dot(left, right, preferred_element_type=jnp.float32)]
    pallas_call x1 -> x3, Pallas kernels: 70.4 us -> 270 us  [the longest x1 130 us: rest(): pl.pallas_call(functools.partial(rest_kernel, SLOTS, K, STRIDE), grid=(ro...]
    convert_element_type x8 -> x0, local copies, waits for them, and re-layouts: 47.5 us -> none  [the longest x2 14.1 us: whole_chains(): jnp.einsum('chqk,cqhd->ckhd', probs_low, grad_context, preferred_element_...]
    reshape x8 -> x3, local copies, waits for them, and re-layouts: 49 us -> 3.72 us  [whole_chains(): row = lambda a: a.reshape(1, -1)]
    reduce_sum x8 -> x0, other arithmetic: 25.9 us -> none  [the longest x1 10.5 us: whole_chains(): jnp.sum(jnp.exp(scores - highest), axis=-1, keepdims=True)]
    convert_element_type x14 -> x4, other arithmetic: 22.8 us -> 5.22 us  [whole_chains(): w = {name: part.astype(f32) for name, part in unpack_half(summed).items()}]
    all_gather x7 -> x0, blocking collectives: 14.8 us -> none  [whole_chains(): gather = lambda a, axis: lax.all_gather(a, 'tensor', axis=axis, tiled=True)]
    unnamed x119 -> x22, local copies, waits for them, and re-layouts: 22.9 us -> 8.16 us
  transfers between devices with their start and end apart: 2 -> 0, of which waited for: 0 -> 0; matrix products, arithmetic and copies ran while one was open for 29% -> 0% of each run, Pallas kernels for 0% -> 0%
where the time goes in v2:
time: 289 us; the launch traced here: 294 us
  Pallas kernels  270 us (93%)
  local copies, waits for them, and re-layouts  17.3 us (6%)
  other arithmetic  5.22 us (2%)
    pallas_call x1, Pallas kernels, rest(): pl.pallas_call(functools.partial(rest_kernel, SLOTS, K, STRIDE), grid=(ro...  130 us
    pallas_call x1, Pallas kernels, gather(): pl.pallas_call(gather_kernel, grid=(rows // block,), in_specs=[tile, whol...  75.5 us
    pallas_call x1, Pallas kernels, live_rows(): pl.pallas_call(live_kernel, grid_spec=pltpu.PrefetchScalarGridSpec(num_sc...  65.3 us
    unnamed x22, local copies, waits for them, and re-layouts  8.16 us

profile of v2, /device:TPU:0, one launch (start us, length us, event | category | flops | bytes accessed | tf_op | source)
XLA Modules:
  0.0 293.9 jit_solution(3220969653561017857)
XLA Ops:
  0.7 1.3 reshape.51.bi_ref
  1.9 1.2 reshape.49.bq_ref
  3.2 1.2 reshape.50.bv_ref
  4.4 0.0 copy-start.6
  4.4 0.0 copy-start.7
  4.4 75.5 %gather.1 = (bf16[2240,512]{1,0:T(8,128)(2,1)}, bf16[2240,512]{1,0:T(8,128)(2,1)}, bf16[2240,512]{1,0:T(8,128)(2,1)}, bf16[2,3,512,256]{3,2,1,0:T(8,128)(2,1)}, ...) custom-call(bf16[2240,512]{1,0:T(8,128)(2,1)} %x_ref.5, ...), custom_call_target="tpu_custom_call" | custom-call | tf_op jit(solution)/shard_map/gather/pallas_call | solution.py:449
  79.9 0.0 copy-done.2
  79.9 0.0 copy-done.3
  79.9 0.0 copy-done.4
  79.9 0.0 copy-done.5
  80.0 0.0 copy-done.6
  80.0 0.0 copy-done.7
  80.0 0.6 stack.31.vec_ref
  80.6 65.3 %live_rows.1 = (bf16[2,3072,512]{2,1,0:T(8,128)(2,1)}, f32[16,512]{1,0:T(8,128)}, bf16[2240,512]{1,0:T(8,128)(2,1)}, bf16[2240,512]{1,0:T(8,128)(2,1)}, bf16[2240,512]{1,0:T(8,128)(2,1)}, /*index=5*/f32[2240,512]{1,0:T(8,128)}) custom-call(s32[28]{0:T(128)} %len_ref.1, s32[28]{0:T(128)} %start_ref.1, s32[28]{0:T(128)} %end_ref.1, bf16[2240,512]{1,0:T(8,128)(2,1)} %x_ref.5, ...), custom_call_target="tpu_custom_call" | custom-call | tf_op jit(solution)/shard_map/live_rows/pallas_call | solution.py:720
  146.0 0.0 copy-done.8
  146.0 0.1 dynamic_slice.16
  146.1 0.1 broadcast_in_dim.10
  146.2 0.1 broadcast_in_dim.11
  146.2 1.4 broadcast_in_dim.12.len_ref
  147.6 129.7 %rest.1 = (bf16[3072,512]{1,0:T(8,128)(2,1)}, f32[16,512]{1,0:T(8,128)}, bf16[2240,512]{1,0:T(8,128)(2,1)}, f32[2240,512]{1,0:T(8,128)}) custom-call(bf16[2,3072,512]{2,1,0:T(8,128)(2,1)} %get-tuple-element.42.g, f32[16,512]{1,0:T(8,128)} %get-tuple-element.43.small, bf16[2240,512]{1,0:T(8,128)(2,1)} %x_ref.5, bf16[2240,512]{1,0:T(8,128)(2,1)} %get-tuple-element.35.q_ref, ...), custom_call_target="tpu_custom_call" | custom-call | tf_op jit(solution)/shard_map/rest/pallas_call | solution.py:825
  277.3 1.4 fusion
  278.7 0.0 copy-start.1
  278.7 1.6 maximum_convert_fusion
  280.3 0.0 copy-done
  280.3 0.9 maximum_convert_fusion.1
  281.2 0.6 fusion.2
  281.8 0.6 constant_dynamic-slice_fusion
  282.4 1.6 slice_convert_fusion
  284.0 1.2 slice_convert_fusion.1
  285.1 0.6 dynamic_slice.21
  285.7 3.2 %copy.40 = bf16[2240,512]{1,0:T(8,128)(2,1)} copy(bf16[2240,512]{1,0:T(8,128)(2,1)} %get-tuple-element.87) | data formatting | bytes 4587520
  288.9 4.9 %copy.41 = f32[2240,512]{1,0:T(8,128)} copy(f32[2240,512]{1,0:T(8,128)} %get-tuple-element.88) | data formatting | bytes 9175040
  (17 shorter events, 0.1 us)
Async XLA Ops:
  4.4 75.5 %copy-start.2 = (bf16[512]{0:T(512)(128)(2,1)S(1)}, bf16[512]{0:T(512)(128)(2,1)}, u32[]{:S(2)}) copy-start(bf16[512]{0:T(512)(128)(2,1)} %param.31) | copy-start | bytes 3076
  4.4 75.5 %copy-start.3 = (bf16[512]{0:T(512)(128)(2,1)S(1)}, bf16[512]{0:T(512)(128)(2,1)}, u32[]{:S(2)}) copy-start(bf16[512]{0:T(512)(128)(2,1)} %param.32) | copy-start | bytes 3076
  4.4 75.5 %copy-start.4 = (bf16[512]{0:T(512)(128)(2,1)S(1)}, bf16[512]{0:T(512)(128)(2,1)}, u32[]{:S(2)}) copy-start(bf16[512]{0:T(512)(128)(2,1)} %param.33) | copy-start | bytes 3076
  4.4 75.6 %copy-start.5 = (bf16[512]{0:T(512)(128)(2,1)S(1)}, bf16[512]{0:T(512)(128)(2,1)}, u32[]{:S(2)}) copy-start(bf16[512]{0:T(512)(128)(2,1)} %param.37) | copy-start | bytes 3076
  4.4 75.6 %copy-start.6 = (bf16[512]{0:T(512)(128)(2,1)S(1)}, bf16[512]{0:T(512)(128)(2,1)}, u32[]{:S(2)}) copy-start(bf16[512]{0:T(512)(128)(2,1)} %param.38) | copy-start | bytes 3076
  4.4 75.6 %copy-start.7 = (bf16[512]{0:T(512)(128)(2,1)S(1)}, bf16[512]{0:T(512)(128)(2,1)}, u32[]{:S(2)}) copy-start(bf16[512]{0:T(512)(128)(2,1)} %param.39) | copy-start | bytes 3076
  80.6 65.4 %copy-start.8 = (s32[28]{0:T(128)S(1)}, s32[28]{0:T(128)}, u32[]{:S(2)}) copy-start(s32[28]{0:T(128)} %len_ref.1) | copy-start | bytes 340
  277.3 3.0 %copy-start = (bf16[3072,512]{1,0:T(8,128)(2,1)S(1)}, bf16[3072,512]{1,0:T(8,128)(2,1)}, u32[]{:S(2)}) copy-start(bf16[3072,512]{1,0:T(8,128)(2,1)} %get-tuple-element.51) | copy-start | bytes 9437188
  278.7 2.5 copy-start.1
